TPU v7x, 128 devices: a whole 4x4x4 slice. The times are simulated.
128 devices in a mesh: strike: 32 (over y, x, core), depth: 4 (over z).
Axes of the slice: x: 4, y: 4, z: 4, core: 2. Of those that a mesh axis runs over, the one named last changes fastest.
Arguments:
- forward_field: float32 [3, 512, 64, 512], P(None, 'strike', 'depth'), may hold values from -6 to 6
- adjoint_start: float32 [3, 512, 64, 512], P(None, 'strike', 'depth'), may hold values from -6 to 6
- modulus: float32 [512, 64, 512], P('strike', 'depth'), may hold values from 0.5 to 5
- misfit: float32 [3, 32768], P(None, ('strike', 'depth')), may hold values from -24 to 24
- row_owner: int32 [32768, 1], P(('strike', 'depth')), may hold values from 0 to 127; in each aligned block of 256 rows (0 to 255, 256 to 511, ...) at most 8 rows name the same one
- row_cell: int32 [32768], P(('strike', 'depth')), may hold values from 0 to 255
Outputs:
- adjoint: float32 [3, 512, 64, 512], P(None, 'strike', 'depth')
- gradient: float32 [512, 64, 512], P('strike', 'depth')
Inputs may be any that keep to these rules, and one draw needn't show every extreme that they name: `row_owner`: in the rows of one device no owner is named more than 8 times, a bound that some block reaches.
All inputs are finite; a program needn't handle non-finite values.
Results may differ from a plain program's by a relative error of at most 0.0003.
Values sent between devices are 32-bit elements; how exact they have to be, the bound alone decides.
A program may use at most 128 MiB of HBM per device.

v0:
```python
import jax
import jax.numpy as jnp
from jax import lax
from jax.sharding import PartitionSpec as P

ITERS = 3


penalty_weight = 4.0


def with_halo(cells, sides, width):
    for axis, dim in sides:
        count = lax.axis_size(axis)
        ends = count - 1
        head = lax.slice_in_dim(cells, 0, width, axis=dim)
        tail = lax.slice_in_dim(cells, cells.shape[dim] - width, cells.shape[dim], axis=dim)
        cells = jnp.concatenate(
            [
                lax.ppermute(tail, axis, [(i, (i + 1) % count) for i in range(ends)]),
                cells,
                lax.ppermute(head, axis, [((i + 1) % count, i) for i in range(ends)]),
            ],
            axis=dim,
        )
    return cells


def face_moduli(padded, modulus):
    uppers = [padded[2:, 1:-1, 1:-1], padded[1:-1, 2:, 1:-1], padded[1:-1, 1:-1, 2:]]
    lowers = [padded[:-2, 1:-1, 1:-1], padded[1:-1, :-2, 1:-1], padded[1:-1, 1:-1, :-2]]
    upper_coef = [0.5 * (modulus + beside) for beside in uppers]
    lower_coef = [0.5 * (modulus + beside) for beside in lowers]
    fault_mask = (lax.broadcasted_iota(jnp.int32, modulus.shape, 2) == 0).astype(jnp.float32)
    fault_term = penalty_weight * modulus * fault_mask
    diagonal = fault_term
    for number in range(3):
        diagonal = diagonal + upper_coef[number] + lower_coef[number]
    return (upper_coef, lower_coef, fault_term, diagonal)


def apply_operator(padded, field, upper_coef, lower_coef, fault_term):
    uppers = [padded[:, 2:, 1:-1, 1:-1], padded[:, 1:-1, 2:, 1:-1], padded[:, 1:-1, 1:-1, 2:]]
    lowers = [padded[:, :-2, 1:-1, 1:-1], padded[:, 1:-1, :-2, 1:-1], padded[:, 1:-1, 1:-1, :-2]]
    result = fault_term * field
    for number in range(3):
        result = (
            result
            + upper_coef[number] * (field - uppers[number])
            + lower_coef[number] * (field - lowers[number])
        )
    return result


def strain_product(padded):
    diffs = [
        padded[:, 2:, 1:-1, 1:-1] - padded[:, :-2, 1:-1, 1:-1],
        padded[:, 1:-1, 2:, 1:-1] - padded[:, 1:-1, :-2, 1:-1],
        padded[:, 1:-1, 1:-1, 2:] - padded[:, 1:-1, 1:-1, :-2],
    ]
    result = jnp.zeros(padded.shape[1:], jnp.float32)[:-2, :-2, :-2]
    for number in range(3):
        halved = 0.5 * diffs[number]
        result = result - jnp.sum(halved[:3] * halved[3:], axis=0)
    return result


def pad_normal(rimmed):
    return jnp.pad(rimmed, ((0, 0), (0, 0), (0, 0), (1, 1)))


def residual_energy(remain_now, scaled_now):
    return lax.psum(jnp.sum(remain_now * scaled_now), ("strike", "depth"))


def on_device(forward_field, adjoint_start, modulus, misfit, row_owner, row_cell):
    cells_strike, cells_depth, normal_cells = modulus.shape
    patch_cells = cells_strike * cells_depth
    devices = lax.axis_size(("strike", "depth"))
    owner = row_owner[:, 0]
    dense_plane = (
        jnp.zeros((3, devices, patch_cells), jnp.float32).at[:, owner, row_cell].add(misfit)
    )
    local_plane = lax.psum_scatter(
        dense_plane, ("strike", "depth"), scatter_dimension=1, tiled=True
    )[:, 0, :]
    source = jnp.zeros((3, cells_strike, cells_depth, normal_cells), jnp.float32)
    source = source.at[:, :, :, 0].set(local_plane.reshape(3, cells_strike, cells_depth))
    moduli_rimmed = with_halo(modulus, (("strike", 0), ("depth", 1)), 1)
    moduli_padded = jnp.pad(moduli_rimmed, ((0, 0), (0, 0), (1, 1)))
    upper_coef, lower_coef, fault_term, diagonal = face_moduli(moduli_padded, modulus)

    def operate(field):
        rimmed = with_halo(field, (("strike", 1), ("depth", 2)), 1)
        return apply_operator(pad_normal(rimmed), field, upper_coef, lower_coef, fault_term)

    adjoint = adjoint_start
    remain = source - operate(adjoint_start)
    scaled = remain / diagonal
    search = scaled
    energy = residual_energy(remain, scaled)
    for turn_index in range(ITERS):
        applied = operate(search)
        step_len = energy / lax.psum(jnp.sum(search * applied), ("strike", "depth"))
        adjoint = adjoint + step_len * search
        remain = remain - step_len * applied
        if turn_index + 1 < ITERS:
            scaled = remain / diagonal
            fresh = residual_energy(remain, scaled)
            search = scaled + fresh / energy * search
            energy = fresh
    stacked = jnp.concatenate([forward_field, adjoint], 0)
    strain_rimmed = with_halo(stacked, (("strike", 1), ("depth", 2)), 1)
    gradient = strain_product(pad_normal(strain_rimmed))
    return (adjoint, gradient)


def solution(mesh):
    placed = (
        P(None, "strike", "depth", None),
        P(None, "strike", "depth", None),
        P("strike", "depth", None),
        P(None, ("strike", "depth")),
        P(("strike", "depth"), None),
        P(("strike", "depth")),
    )
    return jax.shard_map(
        on_device,
        mesh=mesh,
        in_specs=placed,
        out_specs=(P(None, "strike", "depth", None), P("strike", "depth", None)),
        check_vma=False,
    )
```

profile of v0, /device:TPU:1, one launch (start us, length us, event | category | flops | bytes accessed | tf_op | source)
XLA Modules:
  0.0 1199.5 jit_solution(18288034557642909354)
XLA Ops:
  8.0 3.3 collective-permute-start
  11.4 3.1 collective-permute-start.2
  15.5 1.9 collective-permute-start.1
  17.4 3.6 collective-permute-start.3
  23.3 7.9 broadcast_in_dim.4
  31.1 25.9 %scatter_fusion = f32[3,128,256]{0,2,1:T(8,128)} fusion(f32[3,128,256]{0,2,1:T(8,128)} %broadcast_in_dim.4, s32[256]{0:T(256)S(1)} %bitcast.4, f32[256,3]{1,0:T(8,128)S(1)} %copy.35), kind=kCustom, calls=%fused_computation | custom fusion | flops 768 | bytes 11264 | tf_op jit(solution)/shard_map/scatter-add | solution.py:82
  59.9 4.2 collective-permute-start.6
  67.5 4.3 collective-permute-start.7
  71.8 2.4 add_add_fusion
  74.2 1.8 collective-permute-done.7
  76.7 4.4 select_maximum_fusion.17
  81.1 640.8 %reduce-scatter.2.cloned.1.call-done = f32[3,1,256]{0,2,1:T(8,128)} async-done(((f32[3,128,256]{0,2,1:T(8,128)}), f32[3,1,256]{0,2,1:T(8,128)}) %reduce-scatter.2.cloned.1.call-update) | async-done | bytes 3088 | tf_op jit(solution)/shard_map/reduce_scatter | solution.py:84
  721.9 2.6 copy.36
  724.6 8.3 broadcast_divide_fusion
  733.1 10.6 collective-permute-start.8
  743.7 1.9 collective-permute-start.9
  748.8 4.6 collective-permute-start.11
  756.1 3.2 select_maximum_fusion.13
  759.4 4.6 multiply_reduce_fusion.3
  764.0 63.8 %all-reduce.7 = (f32[]{:T(128)}, f32[]{:T(128)}) all-reduce(f32[]{:T(128)} %get-tuple-element.19, f32[]{:T(128)} %get-tuple-element.18), channel_id=1, replica_groups=mesh['strike'=32,'depth'=4] {'strike','depth'}, use_global_device_ids=true, to_apply=%region_3.4 | all-reduce | flops 2 | bytes 16 | tf_op jit(solution)/shard_map/psum | solution.py:73
  829.2 3.6 multiply_reduce_fusion.2
  832.7 63.0 %psum.44 = f32[]{:T(128)} all-reduce(f32[]{:T(128)} %get-tuple-element.24), channel_id=1, replica_groups=mesh['strike'=32,'depth'=4] {'strike','depth'}, use_global_device_ids=true, to_apply=%region_7.8 | all-reduce | flops 1 | bytes 8 | tf_op jit(solution)/shard_map/psum | solution.py:73
  897.0 2.0 multiply_add_fusion.2
  899.2 2.6 collective-permute-start.12
  901.8 3.0 collective-permute-start.13
  907.9 4.3 collective-permute-start.15
  913.2 2.1 collective-permute-done.15
  915.3 3.2 select_maximum_fusion.9
  918.6 4.5 multiply_reduce_fusion.1
  923.1 67.5 %psum.45 = f32[]{:T(128)} all-reduce(f32[]{:T(128)} %get-tuple-element.22), channel_id=1, replica_groups=mesh['strike'=32,'depth'=4] {'strike','depth'}, use_global_device_ids=true, to_apply=%region_9.10 | all-reduce | flops 1 | bytes 8 | tf_op jit(solution)/shard_map/psum | solution.py:104
  992.0 3.0 multiply_reduce_fusion
  995.0 62.7 %psum.46 = f32[]{:T(128)} all-reduce(f32[]{:T(128)} %multiply_reduce_fusion), channel_id=1, replica_groups=mesh['strike'=32,'depth'=4] {'strike','depth'}, use_global_device_ids=true, to_apply=%region_11.12 | all-reduce | flops 1 | bytes 8 | tf_op jit(solution)/shard_map/psum | solution.py:73
  1059.0 2.7 multiply_add_fusion.1
  1061.9 2.6 collective-permute-start.16
  1064.5 3.0 collective-permute-start.17
  1070.7 4.3 collective-permute-start.19
  1075.9 2.1 collective-permute-done.19
  1078.0 3.2 select_maximum_fusion.5
  1081.3 3.5 fusion.13
  1084.9 2.1 copy.82
  1086.9 67.6 %psum.47 = f32[]{:T(128)} all-reduce(f32[]{:T(128)} %fusion.13), channel_id=1, replica_groups=mesh['strike'=32,'depth'=4] {'strike','depth'}, use_global_device_ids=true, to_apply=%region_13.14 | all-reduce | flops 1 | bytes 8 | tf_op jit(solution)/shard_map/psum | solution.py:104
  1155.8 3.6 multiply_add_fusion
  1159.9 2.6 collective-permute-start.20
  1162.5 3.1 collective-permute-start.21
  1169.7 4.0 collective-permute-start.23
  1173.7 2.1 copy.89
  1179.2 7.1 select_maximum_fusion
  1187.8 2.6 fusion.6
  (139 shorter events, 36.7 us)
Async XLA Ops:
  7.2 714.8 %reduce-scatter.2.cloned.1.call-start = ((), (), s32[]{:S(2)}) async-start(), calls=%async_computation.1 | async-start | bytes 16908288 | tf_op jit(solution)/shard_map/reduce_scatter | solution.py:84
  8.0 50.3 %collective-permute-start = (f32[1,16,512]{2,0,1:T(1,128)S(1)}, f32[1,16,512]{2,0,1:T(1,128)S(1)}, u32[]{:S(2)}, u32[]{:S(2)}) collective-permute-start(f32[1,16,512]{2,0,1:T(1,128)S(1)} %copy.39), channel_id=1, source_target_pairs={{4,0},{8,4},{12,8},{16,12},{20,16},{24,20},{28,24},{32,28},{36,32}... | collective-permute-start | bytes 98312 | tf_op jit(solution)/shard_map/ppermute | solution.py:22
  11.4 47.0 %collective-permute-start.2 = (f32[1,16,512]{2,0,1:T(1,128)S(1)}, f32[1,16,512]{2,0,1:T(1,128)S(1)}, u32[]{:S(2)}, u32[]{:S(2)}) collective-permute-start(f32[1,16,512]{2,0,1:T(1,128)S(1)} %copy.45), channel_id=1, source_target_pairs={{0,4},{4,8},{8,12},{12,16},{16,20},{20,24},{24,28},{28,32},{32,36}... | collective-permute-start | bytes 98312 | tf_op jit(solution)/shard_map/ppermute | solution.py:20
  15.5 50.4 %collective-permute-start.1 = (f32[3,1,16,512]{3,2,1,0:T(8,128)S(1)}, f32[3,1,16,512]{3,2,1,0:T(8,128)S(1)}, u32[]{:S(2)}, u32[]{:S(2)}) collective-permute-start(f32[3,1,16,512]{3,2,1,0:T(8,128)S(1)} %get-tuple-element.58), channel_id=1, source_target_pairs={{4,0},{8,4},{12,8},{16,12},{20,16},{24,20},{28,24},{32,28},{36,32}... | collective-permute-start | bytes 294920 | tf_op jit(solution)/shard_map/ppermute | solution.py:22
  17.4 48.6 %collective-permute-start.3 = (f32[3,1,16,512]{3,2,1,0:T(8,128)S(1)}, f32[3,1,16,512]{3,2,1,0:T(8,128)S(1)}, u32[]{:S(2)}, u32[]{:S(2)}) collective-permute-start(f32[3,1,16,512]{3,2,1,0:T(8,128)S(1)} %get-tuple-element.57), channel_id=1, source_target_pairs={{0,4},{4,8},{8,12},{12,16},{16,20},{20,24},{24,28},{28,32},{32,36}... | collective-permute-start | bytes 294920 | tf_op jit(solution)/shard_map/ppermute | solution.py:20
  58.4 6.6 collective-permute-start.4
  59.9 5.4 collective-permute-start.6
  65.1 11.0 copy-start.4
  66.2 8.0 collective-permute-start.5
  67.5 8.6 collective-permute-start.7
  74.2 685.2 %copy-start.5 = (f32[16,16,512]{2,0,1:T(8,128)}, f32[16,16,512]{2,0,1:T(8,128)S(1)}, u32[]{:S(2)}) copy-start(f32[16,16,512]{2,0,1:T(8,128)S(1)} %get-tuple-element.30) | copy-start | bytes 1572868
  74.2 685.2 %copy-start.8 = (f32[16,16,512]{2,0,1:T(8,128)}, f32[16,16,512]{2,0,1:T(8,128)S(1)}, u32[]{:S(2)}) copy-start(f32[16,16,512]{2,0,1:T(8,128)S(1)} %get-tuple-element.31) | copy-start | bytes 1572868
  74.2 755.0 %copy-start.2 = (f32[16,16,512]{2,0,1:T(8,128)}, f32[16,16,512]{2,0,1:T(8,128)S(1)}, u32[]{:S(2)}) copy-start(f32[16,16,512]{2,0,1:T(8,128)S(1)} %get-tuple-element.29) | copy-start | bytes 1572868
  732.9 164.1 %copy-start = (f32[3,16,16,512]{3,1,2,0:T(8,128)}, f32[3,16,16,512]{3,1,2,0:T(8,128)S(1)}, u32[]{:S(2)}) copy-start(f32[3,16,16,512]{3,1,2,0:T(8,128)S(1)} %get-tuple-element.28) | copy-start | bytes 4718596
  733.1 12.6 %collective-permute-start.8 = (f32[3,1,16,512]{3,2,1,0:T(8,128)S(1)}, f32[3,1,16,512]{3,2,1,0:T(8,128)S(1)}, u32[]{:S(2)}, u32[]{:S(2)}) collective-permute-start(f32[3,1,16,512]{3,2,1,0:T(8,128)S(1)} %copy.63), channel_id=1, source_target_pairs={{4,0},{8,4},{12,8},{16,12},{20,16},{24,20},{28,24},{32,28},{36,32}... | collective-permute-start | bytes 294920 | tf_op jit(solution)/shard_map/ppermute | solution.py:22
  743.7 3.5 collective-permute-start.9
  747.5 7.5 collective-permute-start.10
  748.8 10.6 copy-start.11
  748.8 10.6 copy-start.14
  748.8 10.6 copy-start.17
  748.8 7.3 collective-permute-start.11
  899.2 5.9 collective-permute-start.12
  901.8 4.6 collective-permute-start.13
  906.6 6.6 collective-permute-start.14
  907.9 10.7 copy-start.6
  907.9 10.7 copy-start.9
  907.9 10.7 copy-start.12
  907.9 10.7 copy-start.15
  907.9 10.7 copy-start.18
  907.9 10.7 copy-start.21
  907.9 10.7 copy-start.24
  907.9 7.4 collective-permute-start.15
  918.6 73.4 %copy-start.3 = (f32[16,16,512]{2,0,1:T(8,128)S(1)}, f32[16,16,512]{2,0,1:T(8,128)}, u32[]{:S(2)}) copy-start(f32[16,16,512]{2,0,1:T(8,128)} %copy-done.2) | copy-start | bytes 1572868
  1061.9 5.9 collective-permute-start.16
  1064.5 4.6 collective-permute-start.17
  1069.3 6.6 collective-permute-start.18
  1070.6 10.7 copy-start.7
  1070.6 10.7 copy-start.10
  1070.6 10.7 copy-start.13
  1070.6 10.7 copy-start.16
  1070.6 10.7 copy-start.19
  1070.7 10.7 copy-start.22
  1070.7 10.7 copy-start.25
  1070.7 7.4 collective-permute-start.19
  1159.9 7.0 collective-permute-start.20
  1162.5 5.5 collective-permute-start.21
  1168.4 9.0 collective-permute-start.22
  1169.7 9.5 collective-permute-start.23
  (10 other events, 58.0 us)
Sparse Core Ops, SparseCore 0:
  57.2 664.7 reduce-scatter.1
where the time goes:
time: 1210 us; the launch traced here: 1200 us
  waiting for transfers between devices  662 us (55%)
  blocking collectives  325 us (27%)
  other arithmetic  92.8 us (8%)
  starting transfers between devices  75 us (6%)
  local copies, waits for them, and re-layouts  23.2 us (2%)
  between operations  21.9 us (2%)
    reduce_scatter x1, waiting for transfers between devices, on_device(): lax.psum_scatter(dense_plane, ('strike', 'depth'), scatter_dimension=1, t...  641 us
    psum x3, blocking collectives, residual_energy(): return lax.psum(jnp.sum(remain_now * scaled_now), ('strike', 'depth'))  190 us
    psum x2, blocking collectives, on_device(): step_len = energy / lax.psum(jnp.sum(search * applied), ('strike', 'depth'))  135 us
    ppermute x12, starting transfers between devices, with_halo(): lax.ppermute(tail, axis, [(i, (i + 1) % count) for i in range(ends)])  43.5 us
    ppermute x12, starting transfers between devices, with_halo(): lax.ppermute(head, axis, [((i + 1) % count, i) for i in range(ends)])  31.5 us
    scatter-add x1, other arithmetic, on_device(): jnp.zeros((3, devices, patch_cells), jnp.float32).at[:, owner, row_cell]  25.9 us
  transfers between devices with their start and end apart: 25, of which 18 were waited for; matrix products, arithmetic and copies ran while one was open for 4% of the time, Pallas kernels for 0%

commit v1 on v0

v1 whole, which is shorter than its diff:
```python
import jax
import jax.numpy as jnp
from jax import lax
from jax.experimental import pallas as pl
from jax.experimental.pallas import tpu as pltpu
from jax.sharding import PartitionSpec as P

MESH = pl.DeviceIdType.MESH
C, S, D, N = 3, 16, 16, 512
NS_DEV, ND_DEV = 32, 4
CAP = 8
PENALTY = 4.0
f32 = jnp.float32
FM, FX, FF, F0, F1, F2 = range(6)


def halves(v):
    hi = v.astype(jnp.bfloat16)
    rest = v - hi.astype(f32)
    mid = rest.astype(jnp.bfloat16)
    lo = (rest - mid.astype(f32)).astype(jnp.bfloat16)
    return hi, mid, lo


def lane_low(v):
    return pltpu.roll(v, 1, 1)


def lane_high(v):
    return pltpu.roll(v, N - 1, 1)


def rows_low(v, halo):
    row = lax.broadcasted_iota(jnp.int32, v.shape, 0)
    return jnp.where(row == 0, jnp.broadcast_to(halo, v.shape), pltpu.roll(v, 1, 0))


def rows_high(v, halo):
    row = lax.broadcasted_iota(jnp.int32, v.shape, 0)
    return jnp.where(row == D - 1, jnp.broadcast_to(halo, v.shape), pltpu.roll(v, D - 1, 0))


def kernel(f_hbm, x_hbm, m_hbm, mis_ref, own_ref, cell_ref, adj_ref, grad_ref,
           mb, xb, fb, ub, hm, hx, hf, hu, sm, sx, sf, su, coef, diag, inv,
           msg1, got1, msg2, got2, red, got3, got4,
           load_sem, ssem, rsem, s1, r1, s2, r2, s3, r3, s4, r4):
    si, di = lax.axis_index("strike"), lax.axis_index("depth")
    core, chip = lax.rem(si, 2), si // 2
    near = core * 4 + di

    loads = [
        pltpu.make_async_copy(m_hbm, mb.at[pl.ds(1, S)], load_sem.at[0]),
        pltpu.make_async_copy(x_hbm, xb.at[:, pl.ds(1, S)], load_sem.at[1]),
        pltpu.make_async_copy(f_hbm, fb.at[:, pl.ds(1, S)], load_sem.at[2]),
    ]
    for load in loads:
        load.start()

    def near_dev(k):
        t = lax.rem(near + k, 8)
        return (chip * 2 + t // 4, lax.rem(t, 4)), t

    def far_dev(k):
        t = lax.rem(chip + k, 16)
        return (t * 2 + core, di), t

    strike_up, strike_dn = lax.rem(si + 1, NS_DEV), lax.rem(si + NS_DEV - 1, NS_DEV)
    barrier = pltpu.get_barrier_semaphore()
    for t in (strike_up, strike_dn):
        pl.semaphore_signal(barrier, inc=1, device_id=(t, di), device_id_type=MESH)
    for k in range(1, 8):
        pl.semaphore_signal(barrier, inc=1, device_id=near_dev(k)[0], device_id_type=MESH)
    for k in range(1, 16):
        pl.semaphore_signal(barrier, inc=1, device_id=far_dev(k)[0], device_id_type=MESH)

    @pl.when(si == 0)
    def _():
        mb[0] = jnp.zeros((D, N), f32)
        for buf in (xb, fb):
            buf[:, 0] = jnp.zeros((C, D, N), f32)
        ub[:, :, 0] = jnp.zeros((3, C, D, N), f32)

    @pl.when(si == NS_DEV - 1)
    def _():
        mb[S + 1] = jnp.zeros((D, N), f32)
        for buf in (xb, fb):
            buf[:, S + 1] = jnp.zeros((C, D, N), f32)
        ub[:, :, S + 1] = jnp.zeros((3, C, D, N), f32)

    for edge, side in ((0, 0), (ND_DEV - 1, 1)):
        @pl.when(di == edge)
        def _(side=side):
            hm[side] = jnp.zeros((S, N), f32)
            hx[side] = jnp.zeros((C, S, N), f32)
            hf[side] = jnp.zeros((C, S, N), f32)
            hu[:, side] = jnp.zeros((3, C, S, N), f32)

    owner, cell = own_ref[...], cell_ref[...]
    rows = owner.shape[1]
    same = (lax.broadcasted_iota(jnp.int32, (128, rows), 0) == owner).astype(f32)
    before = (lax.broadcasted_iota(jnp.int32, (rows, rows), 0)
              < lax.broadcasted_iota(jnp.int32, (rows, rows), 1)).astype(f32).astype(jnp.bfloat16)
    count = jnp.dot(same.astype(jnp.bfloat16), before, preferred_element_type=f32)
    rank = jnp.sum(same * count, axis=0, keepdims=True)
    place = owner * CAP + rank.astype(jnp.int32)
    values = jnp.concatenate([mis_ref[...], cell.astype(f32), jnp.zeros((4, rows), f32)], axis=0)
    parts = jnp.concatenate([p.astype(f32) for p in halves(values)], axis=0).astype(jnp.bfloat16)
    slots = 8 * CAP
    for q in range(16):
        hot = (lax.broadcasted_iota(jnp.int32, (slots, rows), 0) + q * slots == place).astype(f32)
        out = lax.dot_general(parts, hot.astype(jnp.bfloat16), (((1,), (1,)), ((), ())),
                              preferred_element_type=f32)
        msg1[q, :, 0:slots] = (out[0:8] + out[8:16] + out[16:24])[0:4]
        msg1[q, :, slots:128] = jnp.zeros((4, 128 - slots), f32)

    def halo_copies(field):
        if field == FM:
            buf, halo, stage = mb, hm, sm
            lane = (lambda i: buf.at[i])
        elif field == FX:
            buf, halo, stage = xb, hx, sx
            lane = (lambda i: buf.at[:, i])
        elif field == FF:
            buf, halo, stage = fb, hf, sf
            lane = (lambda i: buf.at[:, i])
        else:
            k = field - F0
            buf, halo, stage = ub, hu.at[k], su.at[k]
            lane = (lambda i: buf.at[k, :, i])

        def copy(src, dst, way, t):
            return pltpu.make_async_remote_copy(src_ref=src, dst_ref=dst, send_sem=ssem.at[field, way],
                                                recv_sem=rsem.at[field, way], device_id=t, device_id_type=MESH)

        return [
            (di < ND_DEV - 1, di > 0, copy(stage.at[1], halo.at[0], 0, (si, lax.rem(di + 1, ND_DEV)))),
            (di > 0, di < ND_DEV - 1, copy(stage.at[0], halo.at[1], 1, (si, lax.rem(di + ND_DEV - 1, ND_DEV)))),
            (si < NS_DEV - 1, si > 0, copy(lane(S), lane(0), 2, (strike_up, di))),
            (si > 0, si < NS_DEV - 1, copy(lane(1), lane(S + 1), 3, (strike_dn, di))),
        ]

    def send(field):
        for has, _, copy in halo_copies(field):
            pl.when(has)(copy.start)

    def recv(field):
        for _, gets, copy in halo_copies(field):
            pl.when(gets)(copy.wait_recv)

    def sent(field):
        for has, _, copy in halo_copies(field):
            pl.when(has)(copy.wait_send)

    def stage_rows(read, stage):
        for s in range(S):
            v = read(s)
            for c in range(C):
                stage[0, c, s:s + 1] = v[c, 0:1]
                stage[1, c, s:s + 1] = v[c, D - 1:D]

    loads[0].wait()
    for s in range(S):
        sm[0, s:s + 1] = mb[s + 1, 0:1]
        sm[1, s:s + 1] = mb[s + 1, D - 1:D]
    loads[1].wait()
    stage_rows(lambda s: xb[:, s + 1], sx)
    pl.semaphore_wait(barrier, 24)
    send(FM)
    send(FX)

    def far_copy(k):
        (t, idx) = far_dev(k)
        return pltpu.make_async_remote_copy(src_ref=msg1.at[idx], dst_ref=got1.at[chip], send_sem=s1.at[k],
                                            recv_sem=r1.at[k], device_id=t, device_id_type=MESH)

    for k in range(1, 16):
        far_copy(k).start()
    got1[chip] = msg1[chip]
    loads[2].wait()
    stage_rows(lambda s: fb[:, s + 1], sf)
    for k in range(1, 16):
        far_copy(k).wait_recv()

    slot_lane = lax.broadcasted_iota(jnp.int32, (1, 128), 1)
    total = jnp.zeros((3 * 3 * 64, 128), f32)
    for half in range(2):
        offs, picks = [], []
        for q in range(8 * half, 8 * half + 8):
            row = got1[q]
            at = row[3:4].astype(jnp.int32)
            brick = slot_lane // CAP
            at_s = (brick // 4) * S + at // D
            at_d = lax.rem(brick, 4) * D + lax.rem(at, D)
            live = slot_lane < slots
            picks.append((jnp.where(live, at_s, -1), jnp.where(live, at_d, -1), row))
        hot_s = jnp.concatenate([(lax.broadcasted_iota(jnp.int32, (128, 128), 0) == p[0]).astype(f32) for p in picks],
                                axis=1).astype(jnp.bfloat16)
        lines = []
        is_d = [lax.broadcasted_iota(jnp.int32, (64, 128), 0) == p[1] for p in picks]
        vals = [[part.astype(f32) for part in halves(p[2])] for p in picks]
        for c in range(C):
            for part in range(3):
                lines.append(jnp.concatenate(
                    [jnp.where(is_d[j], vals[j][part][c:c + 1], 0.0) for j in range(8)], axis=1))
        left = jnp.concatenate(lines, axis=0).astype(jnp.bfloat16)
        total = total + lax.dot_general(left, hot_s, (((1,), (1,)), ((), ())), preferred_element_type=f32)
    for c in range(C):
        dense = total[(3 * c) * 64:(3 * c + 1) * 64] + total[(3 * c + 1) * 64:(3 * c + 2) * 64] \
            + total[(3 * c + 2) * 64:(3 * c + 3) * 64]
        for t in range(8):
            part = dense[(t % 4) * D:(t % 4 + 1) * D]
            msg2[t, c] = part if t < 4 else pltpu.roll(part, 128 - S, 1)

    def near_copy(src, dst, send_sem, recv_sem, k, t):
        return pltpu.make_async_remote_copy(src_ref=src, dst_ref=dst, send_sem=send_sem.at[k],
                                            recv_sem=recv_sem.at[k], device_id=t, device_id_type=MESH)

    def plane_copy(k):
        t, idx = near_dev(k)
        return near_copy(msg2.at[idx], got2.at[near], s2, r2, k, t)

    for k in range(1, 8):
        plane_copy(k).start()
    got2[near] = msg2[near]

    recv(FM)
    first = lax.broadcasted_iota(jnp.int32, (D, N), 1) == 0
    last = lax.broadcasted_iota(jnp.int32, (D, N), 1) == N - 1

    def coefs(s, _):
        m = mb[s + 1]
        beside = [mb[s], mb[s + 2], rows_low(m, hm[0, pl.ds(s, 1)]), rows_high(m, hm[1, pl.ds(s, 1)]),
                  jnp.where(first, 0.0, lane_low(m)), jnp.where(last, 0.0, lane_high(m))]
        face = [0.5 * (m + b) for b in beside]
        dd = jnp.where(first, PENALTY * m, 0.0)
        for a in face:
            dd = dd + a
        ii = 1.0 / dd
        diag[s] = dd
        inv[s] = ii
        row = lax.broadcasted_iota(jnp.int32, (D, N), 0)
        outside = [(s + si == 0), (s + si == S - 1 + NS_DEV - 1), (row == 0) & (di == 0),
                   (row == D - 1) & (di == ND_DEV - 1), first, last]
        for j in range(6):
            if j < 2:
                coef[j, s] = face[j] * ii
            else:
                coef[j, s] = jnp.where(outside[j], 0.0, face[j] * ii)
        return 0

    lax.fori_loop(0, S, coefs, 0)

    def sweep(read, halo, c, s):
        v = read(c, s + 1)
        out = coef[0, s] * read(c, s) + coef[1, s] * read(c, s + 2)
        out = out + coef[2, s] * rows_low(v, halo[0, c, pl.ds(s, 1)]) + coef[3, s] * rows_high(v, halo[1, c, pl.ds(s, 1)])
        return v, out + coef[4, s] * lane_low(v) + coef[5, s] * lane_high(v)

    recv(FX)

    def start_field(s, _):
        for c in range(C):
            v, w = sweep(lambda c, i: xb[c, i], hx, c, s)
            ub[0, c, s + 1] = w - v
        return 0

    lax.fori_loop(0, S, start_field, 0)
    for k in range(1, 8):
        plane_copy(k).wait_recv()
    lane0 = lax.broadcasted_iota(jnp.int32, (D, 128), 1) == 0
    for c in range(C):
        plane = got2[0, c]
        for j in range(1, 8):
            plane = plane + got2[j, c]
        for s in range(S):
            mine = plane if s == 0 else pltpu.roll(plane, 128 - s, 1)
            ub[0, c, s + 1, :, 0:128] += jnp.where(lane0, mine * inv[s, :, 0:128], 0.0)

    def fold(v):
        w = v[0:8] + v[8:16]
        return w[:, 0:128] + w[:, 128:256] + w[:, 256:384] + w[:, 384:512]

    zero8 = jnp.zeros((8, 128), f32)
    for k in range(3):
        stage_rows(lambda s, k=k: ub[k, :, s + 1], su.at[k])
        send(F0 + k)
        if k == 2:
            send(FF)
        recv(F0 + k)

        def step(s, sums, k=k):
            sums = list(sums)
            dd = diag[s]
            for c in range(C):
                v, w = sweep(lambda c, i: ub[k, c, i], hu.at[k], c, s)
                if k < 2:
                    ub[k + 1, c, s + 1] = w
                du = dd * v
                diff = v - w
                sums[0] = sums[0] + fold(du * v)
                sums[1] = sums[1] + fold(du * diff)
                sums[2] = sums[2] + fold(dd * (w * diff))
                sums[3] = sums[3] + fold(du * w)
            return tuple(sums)

        got = lax.fori_loop(0, S, step, (zero8,) * 4)
        for j in range(4):
            red[0, pl.ds(4 * k + j, 1)] = jnp.sum(got[j], axis=0, keepdims=True)
    red[0, pl.ds(12, 4)] = jnp.zeros((4, 128), f32)

    got3[chip] = red[0]

    def sum_copy(k):
        t, _ = far_dev(k)
        return near_copy(red.at[0], got3.at[chip], s3, r3, k, t)

    for k in range(1, 16):
        sum_copy(k).start()
    for k in range(1, 16):
        sum_copy(k).wait_recv()
    part = got3[0]
    for j in range(1, 16):
        part = part + got3[j]
    red[1] = part
    got4[near] = part

    def last_copy(k):
        t, _ = near_dev(k)
        return near_copy(red.at[1], got4.at[near], s4, r4, k, t)

    for k in range(1, 8):
        last_copy(k).start()
    for k in range(1, 8):
        last_copy(k).wait_recv()
    part = got4[0]
    for j in range(1, 8):
        part = part + got4[j]
    tot = jnp.sum(part, axis=1, keepdims=True)

    def at(i):
        return tot[i:i + 1]

    b0, b1, b2 = at(0), at(3), at(4)
    g0, g1, g2, g3, g4 = at(1), at(2), at(5), at(6), at(9)
    l1, l2 = g1 / g0, g2 / g0
    s11, s12, s22 = g2 - l1 * g1, g3 - l1 * g2, g4 - l2 * g2
    y1, y2 = b1 - l1 * b0, b2 - l2 * b0
    l3 = s12 / s11
    c2 = (y2 - l3 * y1) / (s22 - l3 * s12)
    c1 = (y1 - s12 * c2) / s11
    c0 = (b0 - g1 * c1 - g2 * c2) / g0

    def combine(x, u):
        return x + c0 * u[0] + c1 * u[1] + c2 * u[2]

    recv(FF)
    sent(FX)

    def adjoint_cells(s, _):
        for c in range(C):
            xb[c, s] = combine(xb[c, s], [ub[k, c, s] for k in range(3)])
        return 0

    lax.fori_loop(0, S + 2, adjoint_cells, 0)
    for side in range(2):
        for c in range(C):
            hx[side, c] = combine(hx[side, c], [hu[k, side, c] for k in range(3)])

    def gradient_cells(s, _):
        total = jnp.zeros((D, N), f32)
        for c in range(C):
            a, b = xb[c, s + 1], fb[c, s + 1]
            adj_ref[c, s] = a
            da = xb[c, s + 2] - xb[c, s]
            db = fb[c, s + 2] - fb[c, s]
            total = total + da * db
            da = rows_high(a, hx[1, c, pl.ds(s, 1)]) - rows_low(a, hx[0, c, pl.ds(s, 1)])
            db = rows_high(b, hf[1, c, pl.ds(s, 1)]) - rows_low(b, hf[0, c, pl.ds(s, 1)])
            total = total + da * db
            da = jnp.where(last, 0.0, lane_high(a)) - jnp.where(first, 0.0, lane_low(a))
            db = jnp.where(last, 0.0, lane_high(b)) - jnp.where(first, 0.0, lane_low(b))
            total = total + da * db
        grad_ref[s] = -0.25 * total
        return 0

    lax.fori_loop(0, S, gradient_cells, 0)
    for k in range(1, 16):
        far_copy(k).wait_send()
        sum_copy(k).wait_send()
    for k in range(1, 8):
        plane_copy(k).wait_send()
        last_copy(k).wait_send()
    for field in (FM, FF, F0, F1, F2):
        sent(field)


def on_device(forward_field, adjoint_start, modulus, misfit, row_owner, row_cell):
    rows = row_cell.shape[0]
    vm = pltpu.VMEM
    dma = pltpu.SemaphoreType.DMA
    field = vm((C, S + 2, D, N), f32)
    face = vm((2, C, S, N), f32)
    anywhere, inside = pl.BlockSpec(memory_space=pl.ANY), pl.BlockSpec(memory_space=pltpu.VMEM)
    return pl.pallas_call(
        kernel,
        out_shape=(jax.ShapeDtypeStruct((C, S, D, N), f32), jax.ShapeDtypeStruct((S, D, N), f32)),
        in_specs=[anywhere] * 3 + [inside] * 3,
        out_specs=(inside, inside),
        scratch_shapes=[
            vm((S + 2, D, N), f32), field, field, vm((3, C, S + 2, D, N), f32),
            vm((2, S, N), f32), face, face, vm((3, 2, C, S, N), f32),
            vm((2, S, N), f32), face, face, vm((3, 2, C, S, N), f32),
            vm((6, S, D, N), f32), vm((S, D, N), f32), vm((S, D, N), f32),
            vm((16, 4, 128), f32), vm((16, 4, 128), f32),
            vm((8, C, D, 128), f32), vm((8, C, D, 128), f32),
            vm((2, 16, 128), f32), vm((16, 16, 128), f32), vm((8, 16, 128), f32),
            dma((3,)), dma((6, 4)), dma((6, 4)),
            dma((16,)), dma((16,)), dma((8,)), dma((8,)), dma((16,)), dma((16,)), dma((8,)), dma((8,)),
        ],
        compiler_params=pltpu.CompilerParams(collective_id=0, has_side_effects=True, vmem_limit_bytes=48 << 20),
        name="window",
    )(forward_field, adjoint_start, modulus, misfit, row_owner.reshape(1, rows), row_cell.reshape(1, rows))


def solution(mesh):
    placed = (
        P(None, "strike", "depth", None),
        P(None, "strike", "depth", None),
        P("strike", "depth", None),
        P(None, ("strike", "depth")),
        P(("strike", "depth"), None),
        P(("strike", "depth")),
    )
    return jax.shard_map(
        on_device,
        mesh=mesh,
        in_specs=placed,
        out_specs=(P(None, "strike", "depth", None), P("strike", "depth", None)),
        check_vma=False,
    )
```

time: 1210 us -> 62.1 us (0.05)
  waiting for transfers between devices: 662 us -> 0 us
  blocking collectives: 325 us -> 0 us
  other arithmetic: 92.8 us -> 0 us
  starting transfers between devices: 75 us -> 0 us
  Pallas kernels: 0 us -> 53.4 us
  between operations: 21.9 us -> 0.65 us
  local copies, waits for them, and re-layouts: 23.2 us -> 7.83 us
    reduce_scatter x1 -> x0, waiting for transfers between devices: 641 us -> none  [on_device(): lax.psum_scatter(dense_plane, ('strike', 'depth'), scatter_dimension=1, t...]
    psum x5 -> x0, blocking collectives: 325 us -> none  [the longest x3 190 us: residual_energy(): return lax.psum(jnp.sum(remain_now * scaled_now), ('strike', 'depth'))]
    ppermute x24 -> x0, starting transfers between devices: 75 us -> none  [the longest x12 43.5 us: with_halo(): lax.ppermute(tail, axis, [(i, (i + 1) % count) for i in range(ends)])]
    pallas_call x0 -> x1, Pallas kernels: none -> 53.4 us  [on_device(): pl.pallas_call(kernel, out_shape=(jax.ShapeDtypeStruct((C, S, D, N), f32)...]
    scatter-add x1 -> x0, other arithmetic: 25.9 us -> none  [on_device(): jnp.zeros((3, devices, patch_cells), jnp.float32).at[:, owner, row_cell]]
    concatenate x14 -> x0, other arithmetic: 23.1 us -> none  [the longest x12 22 us: with_halo(): jnp.concatenate([lax.ppermute(tail, axis, [(i, (i + 1) % count) for i in...]
    ppermute x24 -> x0, waiting for transfers between devices: 21.1 us -> none  [the longest x12 14 us: with_halo(): lax.ppermute(tail, axis, [(i, (i + 1) % count) for i in range(ends)])]
    reduce_sum x7 -> x0, other arithmetic: 20.3 us -> none  [the longest x3 12.6 us: on_device(): step_len = energy / lax.psum(jnp.sum(search * applied), ('strike', 'depth'))]
  transfers between devices with their start and end apart: 25 -> 0, of which waited for: 18 -> 0; matrix products, arithmetic and copies ran while one was open for 4% -> 0% of each run, Pallas kernels for 0% -> 0%
where the time goes in v1:
time: 62.1 us; the launch traced here: 61.9 us
  Pallas kernels  53.4 us (86%)
  local copies, waits for them, and re-layouts  7.83 us (13%)
  between operations  0.65 us (1%)
    pallas_call x1, Pallas kernels, on_device(): pl.pallas_call(kernel, out_shape=(jax.ShapeDtypeStruct((C, S, D, N), f32)...  53.4 us
    unnamed x14, local copies, waits for them, and re-layouts  7.83 us

profile of v1, /device:TPU:1, one launch (start us, length us, event | category | flops | bytes accessed | tf_op | source)
XLA Modules:
  0.0 61.9 jit_solution(4156940102010396717)
XLA Ops:
  0.6 0.0 copy-start
  0.6 1.4 %copy-done = f32[3,16,16,512]{3,2,1,0:T(8,128)S(1)} copy-done((f32[3,16,16,512]{3,2,1,0:T(8,128)S(1)}, f32[3,16,16,512]{3,2,1,0:T(8,128)}, u32[]{:S(2)}) %copy-start) | copy-done | bytes 1572888
  2.0 0.0 copy-start.1
  2.0 1.4 %copy-done.1 = f32[3,16,16,512]{3,2,1,0:T(8,128)S(1)} copy-done((f32[3,16,16,512]{3,2,1,0:T(8,128)S(1)}, f32[3,16,16,512]{3,2,1,0:T(8,128)}, u32[]{:S(2)}) %copy-start.1) | copy-done | bytes 1572888
  3.4 0.0 copy-start.2
  3.5 1.0 %copy-done.2 = f32[16,16,512]{2,1,0:T(8,128)S(1)} copy-done((f32[16,16,512]{2,1,0:T(8,128)S(1)}, f32[16,16,512]{2,1,0:T(8,128)}, u32[]{:S(2)}) %copy-start.2) | copy-done | bytes 524312
  4.5 0.0 copy-start.3
  4.5 0.7 %copy-done.3 = f32[3,256]{1,0:T(4,128)S(1)} copy-done((f32[3,256]{1,0:T(4,128)S(1)}, f32[3,256]{1,0:T(4,128)}, u32[]{:S(2)}) %copy-start.3) | copy-done | bytes 3096
  5.2 0.0 copy-start.4
  5.2 0.7 %copy-done.4 = s32[256,1]{0,1:T(1,128)S(1)} copy-done((s32[256,1]{0,1:T(1,128)S(1)}, s32[256,1]{0,1:T(1,128)}, u32[]{:S(2)}) %copy-start.4) | copy-done | bytes 1048
  5.9 0.0 copy-start.5
  5.9 0.7 %copy-done.5 = s32[256]{0:T(256)S(1)} copy-done((s32[256]{0:T(256)S(1)}, s32[256]{0:T(256)}, u32[]{:S(2)}) %copy-start.5) | copy-done | bytes 1048
  6.5 53.4 %window.1 = (f32[3,16,16,512]{3,2,1,0:T(8,128)S(1)}, f32[16,16,512]{2,1,0:T(8,128)S(1)}) custom-call(f32[3,16,16,512]{3,2,1,0:T(8,128)S(1)} %copy-done, f32[3,16,16,512]{3,2,1,0:T(8,128)S(1)} %copy-done.1, f32[16,16,512]{2,1,0:T(8,128)S(1)} %copy-done.2, f32[3,256]{1,0:T(4,128)S(1)} %copy-done.3, s32[1,256]{1,0:T(1,128)S(1)} %bitcast.2, s32[1,256]{1,0:T(1,128)S(1)} %bitcast.3), custom_call_target="tpu_custom_call" | custom-call | tf_op jit(solution)/shard_map/window/pallas_call | solution.py:404
  59.9 1.1 %copy.10 = f32[3,16,16,512]{3,2,1,0:T(8,128)} copy(f32[3,16,16,512]{3,2,1,0:T(8,128)S(1)} %get-tuple-element.4) | data formatting | bytes 3145728
  61.1 0.8 %copy.11 = f32[16,16,512]{2,1,0:T(8,128)} copy(f32[16,16,512]{2,1,0:T(8,128)S(1)} %get-tuple-element.5) | data formatting | bytes 1048576
Async XLA Ops:
  0.6 1.4 %copy-start = (f32[3,16,16,512]{3,2,1,0:T(8,128)S(1)}, f32[3,16,16,512]{3,2,1,0:T(8,128)}, u32[]{:S(2)}) copy-start(f32[3,16,16,512]{3,2,1,0:T(8,128)} %f_hbm.1) | copy-start | bytes 4718596
  2.0 1.4 %copy-start.1 = (f32[3,16,16,512]{3,2,1,0:T(8,128)S(1)}, f32[3,16,16,512]{3,2,1,0:T(8,128)}, u32[]{:S(2)}) copy-start(f32[3,16,16,512]{3,2,1,0:T(8,128)} %x_hbm.1) | copy-start | bytes 4718596
  3.4 1.0 %copy-start.2 = (f32[16,16,512]{2,1,0:T(8,128)S(1)}, f32[16,16,512]{2,1,0:T(8,128)}, u32[]{:S(2)}) copy-start(f32[16,16,512]{2,1,0:T(8,128)} %m_hbm.1) | copy-start | bytes 1572868
  4.5 0.7 %copy-start.3 = (f32[3,256]{1,0:T(4,128)S(1)}, f32[3,256]{1,0:T(4,128)}, u32[]{:S(2)}) copy-start(f32[3,256]{1,0:T(4,128)} %mis_ref.1) | copy-start | bytes 9220
  5.2 0.7 %copy-start.4 = (s32[256,1]{0,1:T(1,128)S(1)}, s32[256,1]{0,1:T(1,128)}, u32[]{:S(2)}) copy-start(s32[256,1]{0,1:T(1,128)} %param.10) | copy-start | bytes 3076
  5.9 0.7 %copy-start.5 = (s32[256]{0:T(256)S(1)}, s32[256]{0:T(256)}, u32[]{:S(2)}) copy-start(s32[256]{0:T(256)} %param.11) | copy-start | bytes 3076

commit v2 on v0

v2 whole, which is shorter than its diff:
```python
import jax
import jax.numpy as jnp
from jax import lax
from jax.experimental import pallas as pl
from jax.experimental.pallas import tpu as pltpu
from jax.sharding import PartitionSpec as P

MESH = pl.DeviceIdType.MESH
C, S, D, N = 3, 16, 16, 512
NS_DEV, ND_DEV = 32, 4
CAP = 8
PENALTY = 4.0
f32, bf16, i32 = jnp.float32, jnp.bfloat16, jnp.int32
UNROLL = 4


def iota(shape, dim):
    return lax.broadcasted_iota(i32, shape, dim)


def thirds(v):
    hi = v.astype(bf16)
    rest = v - hi.astype(f32)
    mid = rest.astype(bf16)
    return hi, mid, (rest - mid.astype(f32)).astype(bf16)


def cols_low(v):
    return pltpu.roll(v, 1, 1)


def cols_high(v):
    return pltpu.roll(v, N - 1, 1)


def rows_low(v, halo):
    row = iota((8, N), 0)
    top, low = pltpu.roll(v[0:8], 1, 0), pltpu.roll(v[8:16], 1, 0)
    return jnp.concatenate([jnp.where(row == 0, jnp.broadcast_to(halo, (8, N)), top), jnp.where(row == 0, top, low)], 0)


def rows_high(v, halo):
    row = iota((8, N), 0)
    top, low = pltpu.roll(v[0:8], 7, 0), pltpu.roll(v[8:16], 7, 0)
    return jnp.concatenate([jnp.where(row == 7, low, top), jnp.where(row == 7, jnp.broadcast_to(halo, (8, N)), low)], 0)


def fold(v):
    w = v[0:8, 128:N] + v[8:16, 128:N]
    return w[:, 0:128] + w[:, 128:256] + w[:, 256:384]


def window(f_hbm, x_hbm, m_hbm, mis_hbm, own_hbm, cell_hbm, xb, ub, gb, cv,
           mb, fb, mf, xf, ff, uf, ms, xs, fs, us, mc, xc, uc, coef, diag, u3, wb, mis, own, cel,
           msg1, got1, msg2, got2, red, got3, got4,
           load_sem, ssem, rsem, cssem, crsem, wssem, wrsem, s1, r1, s2, r2, s3, r3, s4, r4):
    si, di = lax.axis_index("strike"), lax.axis_index("depth")
    core, chip = lax.rem(si, 2), si // 2
    near = core * 4 + di
    up_s, dn_s = lax.rem(si + 1, NS_DEV), lax.rem(si + NS_DEV - 1, NS_DEV)
    up_d, dn_d = lax.rem(di + 1, ND_DEV), lax.rem(di + ND_DEV - 1, ND_DEV)
    not_first_s, not_last_s = si > 0, si < NS_DEV - 1
    not_first_d, not_last_d = di > 0, di < ND_DEV - 1

    loads = [pltpu.make_async_copy(src, dst, load_sem.at[j]) for j, (src, dst) in enumerate((
        (mis_hbm, mis), (own_hbm, own), (cell_hbm, cel), (m_hbm, mb.at[pl.ds(2, S)]),
        (x_hbm, xb.at[:, pl.ds(2, S)]), (f_hbm, fb.at[:, pl.ds(1, S)])))]
    for load in loads:
        load.start()
    wb[...] = jnp.zeros_like(wb)

    def near_dev(k):
        t = lax.rem(near + k, 8)
        return (chip * 2 + t // 4, lax.rem(t, 4)), t

    def far_dev(k):
        t = lax.rem(chip + k, 16)
        return (t * 2 + core, di), t

    barrier = pltpu.get_barrier_semaphore()
    greet = [far_dev(k)[0] for k in range(1, 16)]
    greet += [(a, b) for a in (up_s, dn_s) for b in (di, up_d, dn_d)]
    greet += [near_dev(k)[0] for k in range(1, 8)]
    for t in greet:
        pl.semaphore_signal(barrier, inc=1, device_id=t, device_id_type=MESH)

    for inside, planes, side in ((not_first_s, 0, 0), (not_last_s, S + 2, 1)):
        @pl.when(jnp.logical_not(inside))
        def _(planes=planes, side=side):
            for j in range(2):
                mb[planes + j] = jnp.zeros((D, N), f32)
                for c in range(C):
                    xb[c, planes + j] = jnp.zeros((D, N), f32)
                    for k in range(3):
                        ub[k, c, planes + j] = jnp.zeros((D, N), f32)
            for c in range(C):
                fb[c, (S + 1) * side] = jnp.zeros((D, N), f32)
            for j in range(6):
                coef[j, S + side] = jnp.zeros((D, N), f32)
            mc[side] = jnp.zeros((2, 8, N), f32)
            xc[side] = jnp.zeros((2, C, 8, N), f32)
            uc[side] = jnp.zeros((2, C, 8, N), f32)
    for inside, side in ((not_first_d, 0), (not_last_d, 1)):
        @pl.when(jnp.logical_not(inside))
        def _(side=side):
            for j in range(6):
                coef[j, S + 2 + side] = jnp.zeros((D, N), f32)
            mf[side] = jnp.zeros((2, S, N), f32)
            for c in range(C):
                xf[c, side] = jnp.zeros((2, S, N), f32)
                ff[c, side] = jnp.zeros((S, N), f32)
                for k in range(3):
                    uf[k, c, side] = jnp.zeros((2, S, N), f32)
            for a in range(2):
                mc[a, side] = jnp.zeros((8, N), f32)
                xc[a, side] = jnp.zeros((C, 8, N), f32)
                uc[a, side] = jnp.zeros((C, 8, N), f32)

    for load in loads[:3]:
        load.wait()
    owner = own[...]
    rows = owner.shape[1]
    same = (iota((128, rows), 0) == owner).astype(f32)
    before = (iota((rows, rows), 0) < iota((rows, rows), 1)).astype(f32).astype(bf16)
    count = jnp.dot(same.astype(bf16), before, preferred_element_type=f32)
    rank = jnp.sum(same * count, axis=0, keepdims=True)
    place = owner * CAP + rank.astype(i32)
    values = jnp.concatenate([mis[...], cel[...].astype(f32), jnp.zeros((4, rows), f32)], axis=0)
    parts = jnp.concatenate([p.astype(f32) for p in thirds(values)], axis=0).astype(bf16)

    def fill(q, _):
        hot = (iota((128, rows), 0) + (q * 64 - 32) == place).astype(f32)
        out = lax.dot_general(parts, hot.astype(bf16), (((1,), (1,)), ((), ())), preferred_element_type=f32)
        msg1[q] = (out[0:8] + out[8:16] + out[16:24])[0:4]
        return 0

    lax.fori_loop(0, 16, fill, 0, unroll=4)

    def stage(read, to, layers):
        for s in range(S):
            v = read(s)
            for layer in range(layers):
                to[0, layer, s:s + 1] = v[layer:layer + 1]
                to[1, layer, s:s + 1] = v[D - 1 - layer:D - layer]

    loads[3].wait()
    stage(lambda s: mb[s + 2], ms, 2)
    col = iota((D, 128), 1)
    for s in range(S):
        tile = mb[s + 2, :, 0:128]
        at = 4 * s + 16
        mask = (col >= at) & (col < at + 4)
        wb[1, 0, 8:24] += jnp.where(mask, pltpu.roll(tile, at, 1), 0.0)
        wb[1, 1, 8:24] += jnp.where(mask, pltpu.roll(tile, at - 1, 1), 0.0)
    loads[4].wait()
    for c in range(C):
        stage(lambda s, c=c: xb[c, s + 2], xs.at[c], 2)
    loads[5].wait()
    for c in range(C):
        for s in range(S):
            fs[c, 0, s:s + 1] = fb[c, s + 1, 0:1]
            fs[c, 1, s:s + 1] = fb[c, s + 1, D - 1:D]

    def remote(src, dst, send_sem, recv_sem, t):
        return pltpu.make_async_remote_copy(src_ref=src, dst_ref=dst, send_sem=send_sem, recv_sem=recv_sem,
                                            device_id=t, device_id_type=MESH)

    def edges(number, buf, face, edge):
        def sems(way):
            return ssem.at[number, way], rsem.at[number, way]
        return [
            (not_last_d, not_first_d, remote(edge.at[1], face.at[0], *sems(0), (si, up_d))),
            (not_first_d, not_last_d, remote(edge.at[0], face.at[1], *sems(1), (si, dn_d))),
            (not_last_s, not_first_s, remote(buf.at[pl.ds(S, 2)], buf.at[pl.ds(0, 2)], *sems(2), (up_s, di))),
            (not_first_s, not_last_s, remote(buf.at[pl.ds(2, 2)], buf.at[pl.ds(S + 2, 2)], *sems(3), (dn_s, di))),
        ]

    def forward_edges():
        def sems(way):
            return ssem.at[7, way], rsem.at[7, way]
        return [
            (not_last_d, not_first_d, remote(fs.at[:, 1], ff.at[:, 0], *sems(0), (si, up_d))),
            (not_first_d, not_last_d, remote(fs.at[:, 0], ff.at[:, 1], *sems(1), (si, dn_d))),
            (not_last_s, not_first_s, remote(fb.at[:, S], fb.at[:, 0], *sems(2), (up_s, di))),
            (not_first_s, not_last_s, remote(fb.at[:, 1], fb.at[:, S + 1], *sems(3), (dn_s, di))),
        ]

    ways = [(1, 1), (1, -1), (-1, 1), (-1, -1)]

    def reach(ps, pd):
        to_s, to_d = (not_last_s if ps > 0 else not_first_s), (not_last_d if pd > 0 else not_first_d)
        from_s, from_d = (not_first_s if ps > 0 else not_last_s), (not_first_d if pd > 0 else not_last_d)
        return to_s & to_d, from_s & from_d, (up_s if ps > 0 else dn_s, up_d if pd > 0 else dn_d)

    def corners(number, source, target):
        out = []
        for way, (ps, pd) in enumerate(ways):
            has, gets, t = reach(ps, pd)
            side, row = (1 if pd > 0 else 0), (S - 1 if ps > 0 else 0)
            a, b = (0 if ps > 0 else 1), (0 if pd > 0 else 1)
            out.append((has, gets, remote(source(side, row), target(a, b), cssem.at[number, way],
                                          crsem.at[number, way], t)))
        return out

    def patches():
        out = []
        for way, (ps, pd) in enumerate([(1, 0), (-1, 0), (0, 1), (0, -1)] + ways):
            if pd == 0:
                has, gets, t = (not_last_s, not_first_s, (up_s, di)) if ps > 0 else (not_first_s, not_last_s, (dn_s, di))
                src, dst = pl.ds(8, 16), pl.ds(8, 16)
            else:
                if ps == 0:
                    has, gets, t = (not_last_d, not_first_d, (si, up_d)) if pd > 0 else (not_first_d, not_last_d, (si, dn_d))
                else:
                    has, gets, t = reach(ps, pd)
                src, dst = (pl.ds(20, 4), pl.ds(4, 4)) if pd > 0 else (pl.ds(8, 4), pl.ds(24, 4))
            out.append((has, gets, remote(wb.at[1, :, src], wb.at[1 - ps, :, dst], wssem.at[way], wrsem.at[way], t)))
        return out

    def m_edges():
        return edges(0, mb, mf, ms) + corners(
            0, lambda side, row: ms.at[side, 0, pl.ds(row, 1)], lambda a, b: mc.at[a, b, pl.ds(0, 1)])

    def x_corners():
        return corners(1, lambda side, row: xs.at[:, side, 0, pl.ds(row, 1)], lambda a, b: xc.at[a, b, :, pl.ds(0, 1)])

    def x_edges(c):
        return edges(1 + c, xb.at[c], xf.at[c], xs.at[c])

    def u_edges(c):
        return edges(4 + c, ub.at[1, c], uf.at[1, c], us.at[c]) + corners(
            2 + c, lambda side, row: us.at[c, side, 0, pl.ds(row, 1)], lambda a, b: uc.at[a, b, c, pl.ds(0, 1)])

    def send(copies):
        for has, _, copy in copies:
            pl.when(has)(copy.start)

    def recv(copies):
        for _, gets, copy in copies:
            pl.when(gets)(copy.wait_recv)

    def sent(copies):
        for has, _, copy in copies:
            pl.when(has)(copy.wait_send)

    def row_copy(k):
        t, idx = far_dev(k)
        return remote(msg1.at[idx], got1.at[chip], s1.at[k], r1.at[k], t)

    def plane_copy(k):
        t, idx = near_dev(k)
        return remote(msg2.at[idx], got2.at[near], s2.at[k], r2.at[k], t)

    def sum_copy(k):
        t, _ = far_dev(k)
        return remote(red.at[0], got3.at[chip], s3.at[k], r3.at[k], t)

    def last_copy(k):
        t, _ = near_dev(k)
        return remote(red.at[1], got4.at[near], s4.at[k], r4.at[k], t)

    pl.semaphore_wait(barrier, len(greet))
    send(m_edges())
    send(x_corners())
    for c in range(C):
        send(x_edges(c))
        if c == 0:
            for k in range(1, 16):
                row_copy(k).start()
    send(patches())
    got1[chip] = msg1[chip]

    first, last = iota((D, N), 1) == 0, iota((D, N), 1) == N - 1

    def coefs(p, m, low, high, row_low, row_high):
        beside = [low, high, rows_low(m, row_low), rows_high(m, row_high),
                  jnp.where(first, 0.0, cols_low(m)), jnp.where(last, 0.0, cols_high(m))]
        face = [0.5 * (m + b) for b in beside]
        dd = jnp.where(first, PENALTY * m, 0.0)
        for a in face:
            dd = dd + a
        ii = 1.0 / dd
        for j in range(6):
            out = face[j] * ii
            if j == 4:
                out = jnp.where(first, 0.0, out)
            if j == 5:
                out = jnp.where(last, 0.0, out)
            coef[j, p] = out
        return dd

    recv(m_edges())

    def own_coefs(s, _):
        diag[s] = coefs(s, mb[s + 2], mb[s + 1], mb[s + 3], mf[0, 0, pl.ds(s, 1)], mf[1, 0, pl.ds(s, 1)])
        return 0

    lax.fori_loop(0, S, own_coefs, 0, unroll=2)
    outer = [not_first_s, not_last_s, not_first_d, not_last_d]

    def corner(cells, a, b):
        return cells(a, b)[0:1]

    def outer_planes(planes, faces, edge, cells):
        return [
            lambda: (planes(1), planes(0), planes(2), corner(cells, 0, 0), corner(cells, 0, 1)),
            lambda: (planes(S + 2), planes(S + 1), planes(S + 3), corner(cells, 1, 0), corner(cells, 1, 1)),
            lambda: (faces(0, 0), faces(0, 1), edge(0), corner(cells, 0, 0), corner(cells, 1, 0)),
            lambda: (faces(1, 0), edge(1), faces(1, 1), corner(cells, 0, 1), corner(cells, 1, 1)),
        ]

    for j, get in enumerate(outer_planes(lambda i: mb[i], lambda a, b: mf[a, b], lambda a: ms[a, 0],
                                         lambda a, b: mc[a, b])):
        @pl.when(outer[j])
        def _(j=j, get=get):
            coefs(S + j, *get())

    def sweep(p, v, low, high, row_low, row_high):
        out = coef[0, p] * low + coef[1, p] * high
        out = out + coef[2, p] * rows_low(v, row_low) + coef[3, p] * rows_high(v, row_high)
        return out + coef[4, p] * cols_low(v) + coef[5, p] * cols_high(v)

    def own_sweep(planes, faces, s):
        v = planes(s + 2)
        return v, sweep(s, v, planes(s + 1), planes(s + 3), faces(0, pl.ds(s, 1)), faces(1, pl.ds(s, 1)))

    def keep_outer(k, c, j, v):
        if j == 0:
            ub[k, c, 1] = v
        elif j == 1:
            ub[k, c, S + 2] = v
        else:
            uf[k, c, j - 2, 0] = v

    zero8 = jnp.zeros((8, 128), f32)
    sums0 = (zero8,) * 3
    sums1 = (zero8,) * 2
    sums2 = (zero8,)

    recv(x_corners())

    def first_half(c, sums):
        recv(x_edges(c))

        def start_field(s, _):
            v, w = own_sweep(lambda i: xb[c, i], lambda a, r: xf[c, a, 0, r], s)
            ub[0, c, s + 2] = w - v
            return 0

        lax.fori_loop(0, S, start_field, 0, unroll=UNROLL)
        for j, get in enumerate(outer_planes(lambda i: xb[c, i], lambda a, b: xf[c, a, b], lambda a: xs[c, a, 0],
                                             lambda a, b: xc[a, b, c])):
            got = get()
            keep_outer(0, c, j, sweep(S + j, *got) - got[0])

        def step(s, sums):
            v, w = own_sweep(lambda i: ub[0, c, i], lambda a, r: uf[0, c, a, 0, r], s)
            ub[1, c, s + 2] = w
            for layer in range(2):
                us[c, 0, layer, pl.ds(s, 1)] = w[layer:layer + 1]
                us[c, 1, layer, pl.ds(s, 1)] = w[D - 1 - layer:D - layer]
            dd = diag[s]
            de = dd * (v - w)
            return (sums[0] + fold(dd * v * v), sums[1] + fold(de * v), sums[2] + fold(de * w))

        sums = lax.fori_loop(0, S, step, sums, unroll=UNROLL)
        send(u_edges(c))
        return sums

    sums0 = first_half(0, sums0)

    for k in range(1, 16):
        row_copy(k).wait_recv()
    slot = iota((1, 128), 1)
    brick_s, brick_d = slot // 32 - 1, lax.rem(slot, 32) // CAP

    def plane_part(half, total):
        hot_d, right = [], [[], [], []]
        for j in range(4):
            row = got1[half * 4 + j]
            at = row[3:4].astype(i32)
            at_s, at_d = brick_s * S + at // D, brick_d * D + lax.rem(at, D) + 8
            hot_d.append((iota((80, 128), 0) == at_d).astype(f32))
            vals = [p.astype(f32) for p in thirds(row)]
            hits = [iota((32, 128), 0) == at_s + (4 - S * o) for o in range(2)]
            for part in range(3):
                lines = []
                for o in range(2):
                    for c in range(C):
                        lines.append(jnp.where(hits[o], vals[part][c:c + 1], 0.0))
                    lines.append(jnp.zeros((32, 128), f32))
                right[part].append(jnp.concatenate(lines, axis=0))
        left = jnp.concatenate(hot_d, axis=1).astype(bf16)
        for part in range(3):
            total = total + lax.dot_general(left, jnp.concatenate(right[part], axis=1).astype(bf16),
                                            (((1,), (1,)), ((), ())), preferred_element_type=f32)
        return total

    dense = jnp.zeros((80, 256), f32)
    for half in range(4):
        dense = plane_part(half, dense)
    for t in range(8):
        msg2[t] = dense[(t % 4) * D:(t % 4) * D + 32, (t // 4) * 128:(t // 4 + 1) * 128]
    for k in range(1, 8):
        plane_copy(k).start()
    got2[near] = msg2[near]

    for c in range(1, C):
        sums0 = first_half(c, sums0)
    send(forward_edges())

    recv(patches())
    lane = iota((32, 128), 1)

    def patch(a):
        low, mid, high = wb[0, a], wb[1, a], wb[2, a]
        return jnp.where(lane < 16, pltpu.roll(low, 64, 1), jnp.where(lane < 80, mid, jnp.where(
            lane < 96, pltpu.roll(high, 64, 1), 0.0)))

    m, above = patch(0), patch(1)
    layer = lax.rem(lane, 4)
    beside = [pltpu.roll(m, 4, 1), pltpu.roll(m, 124, 1), pltpu.roll(m, 1, 0), pltpu.roll(m, 31, 0),
              jnp.where(layer == 0, 0.0, pltpu.roll(m, 1, 1)), above]
    face = [0.5 * (m + b) for b in beside]
    total = jnp.where(layer == 0, PENALTY * m, 0.0)
    for a in face:
        total = total + a
    live = m > 0.0
    ii = jnp.where(live, 1.0 / jnp.where(live, total, 1.0), 0.0)
    face = [a * ii for a in face]
    face[4] = jnp.where(layer == 0, 0.0, face[4])
    face[5] = jnp.where(layer == 3, 0.0, face[5])

    def second_half(c, sums1, sums2):
        recv(u_edges(c))

        def step(s, sums):
            v, w = own_sweep(lambda i: ub[1, c, i], lambda a, r: uf[1, c, a, 0, r], s)
            ub[2, c, s + 2] = w
            de = diag[s] * (v - w)
            return (sums[0] + fold(de * v), sums[1] + fold(de * w))

        sums1 = lax.fori_loop(0, S, step, sums1, unroll=UNROLL)
        for j, get in enumerate(outer_planes(lambda i: ub[1, c, i], lambda a, b: uf[1, c, a, b],
                                             lambda a: us[c, a, 0], lambda a, b: uc[a, b, c])):
            keep_outer(2, c, j, sweep(S + j, *get()))

        def final(s, sums):
            v, w = own_sweep(lambda i: ub[2, c, i], lambda a, r: uf[2, c, a, 0, r], s)
            u3[c, s] = w[:, 0:128]
            return (sums[0] + fold(diag[s] * v * (v - w)),)

        sums2 = lax.fori_loop(0, S, final, sums2, unroll=UNROLL)
        return sums1, sums2

    for c in range(C):
        sums1, sums2 = second_half(c, sums1, sums2)

    for k in range(1, 8):
        plane_copy(k).wait_recv()
    plane = got2[0]
    for j in range(1, 8):
        plane = plane + got2[j]
    spread = ((iota((128, 384), 0) // 32 == iota((128, 384), 1) // 128)
              & (lax.rem(iota((128, 384), 0), 32) * 4 == lax.rem(iota((128, 384), 1), 128))).astype(f32).astype(bf16)
    left = jnp.concatenate([p.astype(f32) for p in thirds(plane)], axis=0).astype(bf16)
    out = jnp.dot(left, spread, preferred_element_type=f32)
    out = out[0:32] + out[32:64] + out[64:96]
    shares = [[out[:, 128 * c:128 * c + 128] * ii for c in range(C)]]
    for k in range(3):
        nxt = []
        for c in range(C):
            w = shares[k][c]
            nxt.append(face[0] * pltpu.roll(w, 4, 1) + face[1] * pltpu.roll(w, 124, 1)
                       + face[2] * pltpu.roll(w, 1, 0) + face[3] * pltpu.roll(w, 31, 0)
                       + face[4] * pltpu.roll(w, 1, 1) + face[5] * pltpu.roll(w, 127, 1))
        shares.append(nxt)

    few = col < 4

    def share(k, c, i):
        return jnp.where(few, pltpu.roll(shares[k][c][8:24], 128 - 4 * (i + 2), 1), 0.0)

    def fold_near(v):
        return v[0:8] + v[8:16]

    for c in range(C):
        sent(u_edges(c))
    sums0, sums1, sums2 = list(sums0), list(sums1), list(sums2)
    for s in range(S):
        dd = diag[s, :, 0:128]
        for c in range(C):
            v = []
            for k in range(3):
                v.append(ub[k, c, s + 2, :, 0:128] + share(k, c, s + 2))
                ub[k, c, s + 2, :, 0:128] = v[k]
            v.append(u3[c, s] + share(3, c, s + 2))
            de = [dd * (v[k] - v[k + 1]) for k in range(3)]
            sums0[0] = sums0[0] + fold_near(dd * v[0] * v[0])
            sums0[1] = sums0[1] + fold_near(de[0] * v[0])
            sums0[2] = sums0[2] + fold_near(de[0] * v[1])
            sums1[0] = sums1[0] + fold_near(de[1] * v[1])
            sums1[1] = sums1[1] + fold_near(de[1] * v[2])
            sums2[0] = sums2[0] + fold_near(de[2] * v[2])
    sums = sums0 + sums1 + sums2
    for j in range(6):
        red[0, j:j + 1] = jnp.sum(sums[j], axis=0, keepdims=True)
    red[0, 6:8] = jnp.zeros((2, 128), f32)

    for k in range(1, 16):
        sum_copy(k).start()
    got3[chip] = red[0]
    for k in range(3):
        for c in range(C):
            for i in (1, S + 2):
                ub[k, c, i, :, 0:128] += share(k, c, i)
            for side, r in ((0, 7), (1, 24)):
                row = jnp.broadcast_to(shares[k][c][r:r + 1], (S, 128))
                row = pltpu.roll(row, 128 - 16, 1)
                for bit in (1, 2, 4, 8):
                    row = jnp.where(iota((S, 128), 0) & bit > 0, pltpu.roll(row, 128 - 4 * bit, 1), row)
                uf[k, c, side, 0, :, 0:128] += jnp.where(few, row, 0.0)
    recv(forward_edges())

    start, end = iota((D, 128), 1) == 0, iota((D, 128), 1) == 127

    def cols_slope(v):
        tiles = [v[:, 128 * j:128 * j + 128] for j in range(4)]
        ups, downs = [pltpu.roll(t, 127, 1) for t in tiles], [pltpu.roll(t, 1, 1) for t in tiles]
        return jnp.concatenate([jnp.where(end, 0.0 if j == 3 else ups[min(j + 1, 3)], ups[j])
                                - jnp.where(start, 0.0 if j == 0 else downs[max(j - 1, 0)], downs[j])
                                for j in range(4)], 1)

    def slopes(p0, p1, p2, row_low, row_high):
        return p2 - p0, rows_high(p1, row_high) - rows_low(p1, row_low), cols_slope(p1)

    def gradients(s, _):
        total = [jnp.zeros((D, N), f32)] * 4
        for c in range(C):
            df = slopes(fb[c, s], fb[c, s + 1], fb[c, s + 2], ff[c, 0, pl.ds(s, 1)], ff[c, 1, pl.ds(s, 1)])
            for k in range(4):
                if k == 0:
                    buf, faces = xb.at[c], xf.at[c]
                else:
                    buf, faces = ub.at[k - 1, c], uf.at[k - 1, c]
                da = slopes(buf[s + 1], buf[s + 2], buf[s + 3], faces[0, 0, pl.ds(s, 1)], faces[1, 0, pl.ds(s, 1)])
                total[k] = total[k] + (df[0] * da[0] + df[1] * da[1] + df[2] * da[2])
        for k in range(4):
            gb[k, s] = -0.25 * total[k]
        return 0

    lax.fori_loop(0, S // 2, gradients, 0)
    for k in range(1, 16):
        sum_copy(k).wait_recv()
    part = got3[0]
    for j in range(1, 16):
        part = part + got3[j]
    red[1] = part
    for k in range(1, 8):
        last_copy(k).start()
    got4[near] = part
    lax.fori_loop(S // 2, S, gradients, 0)
    sent(m_edges())
    sent(x_corners())
    sent(patches())
    sent(forward_edges())
    for c in range(C):
        sent(x_edges(c))
    for k in range(1, 16):
        row_copy(k).wait_send()
        sum_copy(k).wait_send()
    for k in range(1, 8):
        plane_copy(k).wait_send()
    for k in range(1, 8):
        last_copy(k).wait_recv()
    part = got4[0]
    for j in range(1, 8):
        part = part + got4[j]
    tot = jnp.sum(part, axis=1, keepdims=True)

    b0, g0, g1, g2, g3, g4 = [tot[i:i + 1] for i in range(6)]
    b1 = b0 - g0
    b2 = b1 - g1
    l1, l2 = g1 / g0, g2 / g0
    s11, s12, s22 = g2 - l1 * g1, g3 - l1 * g2, g4 - l2 * g2
    y1, y2 = b1 - l1 * b0, b2 - l2 * b0
    l3 = s12 / s11
    c2 = (y2 - l3 * y1) / (s22 - l3 * s12)
    c1 = (y1 - s12 * c2) / s11
    c0 = (b0 - g1 * c1 - g2 * c2) / g0
    for j, v in enumerate((c0, c1, c2)):
        cv[j:j + 1] = jnp.broadcast_to(v, (1, 128))
    for k in range(1, 8):
        last_copy(k).wait_send()


CHUNK = 4


def finish(xb, ub, gb, cv, adj, grad, abuf, gout, sem):
    c = [cv[j:j + 1, 0:1] for j in range(3)]
    copies = []
    for part in range(S // CHUNK):
        for s in range(part * CHUNK, (part + 1) * CHUNK):
            for j in range(C):
                abuf[j, s] = xb[j, s + 2] + c[0] * ub[0, j, s + 2] + c[1] * ub[1, j, s + 2] + c[2] * ub[2, j, s + 2]
            gout[s] = gb[0, s] + c[0] * gb[1, s] + c[1] * gb[2, s] + c[2] * gb[3, s]
        at = pl.ds(part * CHUNK, CHUNK)
        copies.append(pltpu.make_async_copy(abuf.at[:, at], adj.at[:, at], sem.at[0, part]))
        copies.append(pltpu.make_async_copy(gout.at[at], grad.at[at], sem.at[1, part]))
        for copy in copies[-2:]:
            copy.start()
    for copy in copies:
        copy.wait()


def on_device(forward_field, adjoint_start, modulus, misfit, row_owner, row_cell):
    rows = row_cell.shape[0]
    vm, dma = pltpu.VMEM, pltpu.SemaphoreType.DMA
    hbm, inside = pl.BlockSpec(memory_space=pltpu.HBM), pl.BlockSpec(memory_space=pltpu.VMEM)
    shape = jax.ShapeDtypeStruct
    args = [pltpu.with_memory_space_constraint(a, pltpu.HBM) for a in (
        forward_field, adjoint_start, modulus, misfit, row_owner.reshape(1, rows), row_cell.reshape(1, rows))]
    kept = pl.pallas_call(
        window,
        out_shape=(vm((C, S + 4, D, N), f32), vm((3, C, S + 4, D, N), f32), vm((4, S, D, N), f32), vm((8, 128), f32)),
        in_specs=[hbm] * 6,
        out_specs=(inside,) * 4,
        scratch_shapes=[
            vm((S + 4, D, N), f32), vm((C, S + 2, D, N), f32),
            vm((2, 2, S, N), f32), vm((C, 2, 2, S, N), f32), vm((C, 2, S, N), f32), vm((3, C, 2, 2, S, N), f32),
            vm((2, 2, S, N), f32), vm((C, 2, 2, S, N), f32), vm((C, 2, S, N), f32), vm((C, 2, 2, S, N), f32),
            vm((2, 2, 8, N), f32), vm((2, 2, C, 8, N), f32), vm((2, 2, C, 8, N), f32),
            vm((6, S + 4, D, N), f32), vm((S, D, N), f32), vm((C, S, D, 128), f32), vm((3, 2, 32, 128), f32),
            vm((C, rows), f32), vm((1, rows), i32), vm((1, rows), i32),
            vm((16, 4, 128), f32), vm((16, 4, 128), f32), vm((8, 32, 128), f32), vm((8, 32, 128), f32),
            vm((2, 8, 128), f32), vm((16, 8, 128), f32), vm((8, 8, 128), f32),
            dma((6,)), dma((8, 4)), dma((8, 4)), dma((5, 4)), dma((5, 4)), dma((8,)), dma((8,)),
            dma((16,)), dma((16,)), dma((8,)), dma((8,)), dma((16,)), dma((16,)), dma((8,)), dma((8,)),
        ],
        compiler_params=pltpu.CompilerParams(collective_id=0, has_side_effects=True, vmem_limit_bytes=40 << 20),
        name="window",
    )(*args)
    return pl.pallas_call(
        finish,
        out_shape=(shape((C, S, D, N), f32), shape((S, D, N), f32)),
        in_specs=[inside] * 4,
        out_specs=(hbm, hbm),
        scratch_shapes=[vm((C, S, D, N), f32), vm((S, D, N), f32), dma((2, S // CHUNK))],
        compiler_params=pltpu.CompilerParams(vmem_limit_bytes=40 << 20),
        name="finish",
    )(*[pltpu.with_memory_space_constraint(a, pltpu.VMEM) for a in kept])


def solution(mesh):
    placed = (
        P(None, "strike", "depth", None),
        P(None, "strike", "depth", None),
        P("strike", "depth", None),
        P(None, ("strike", "depth")),
        P(("strike", "depth"), None),
        P(("strike", "depth")),
    )
    return jax.shard_map(
        on_device,
        mesh=mesh,
        in_specs=placed,
        out_specs=(P(None, "strike", "depth", None), P("strike", "depth", None)),
        check_vma=False,
    )
```

time: 1210 us -> 38.9 us (0.03)
  waiting for transfers between devices: 662 us -> 0 us
  blocking collectives: 325 us -> 0 us
  other arithmetic: 92.8 us -> 0 us
  starting transfers between devices: 75 us -> 0 us
  Pallas kernels: 0 us -> 38.1 us
  local copies, waits for them, and re-layouts: 23.2 us -> 0 us
  between operations: 21.9 us -> 0.64 us
    reduce_scatter x1 -> x0, waiting for transfers between devices: 641 us -> none  [on_device(): lax.psum_scatter(dense_plane, ('strike', 'depth'), scatter_dimension=1, t...]
    psum x5 -> x0, blocking collectives: 325 us -> none  [the longest x3 190 us: residual_energy(): return lax.psum(jnp.sum(remain_now * scaled_now), ('strike', 'depth'))]
    ppermute x24 -> x0, starting transfers between devices: 75 us -> none  [the longest x12 43.5 us: with_halo(): lax.ppermute(tail, axis, [(i, (i + 1) % count) for i in range(ends)])]
    pallas_call x0 -> x2, Pallas kernels: none -> 38.1 us  [the longest x1 36.6 us: on_device(): pl.pallas_call(window, out_shape=(vm((C, S + 4, D, N), f32), vm((3, C, S...]
    scatter-add x1 -> x0, other arithmetic: 25.9 us -> none  [on_device(): jnp.zeros((3, devices, patch_cells), jnp.float32).at[:, owner, row_cell]]
    concatenate x14 -> x0, other arithmetic: 23.1 us -> none  [the longest x12 22 us: with_halo(): jnp.concatenate([lax.ppermute(tail, axis, [(i, (i + 1) % count) for i in...]
    ppermute x24 -> x0, waiting for transfers between devices: 21.1 us -> none  [the longest x12 14 us: with_halo(): lax.ppermute(tail, axis, [(i, (i + 1) % count) for i in range(ends)])]
    reduce_sum x7 -> x0, other arithmetic: 20.3 us -> none  [the longest x3 12.6 us: on_device(): step_len = energy / lax.psum(jnp.sum(search * applied), ('strike', 'depth'))]
  transfers between devices with their start and end apart: 25 -> 0, of which waited for: 18 -> 0; matrix products, arithmetic and copies ran while one was open for 4% -> 0% of each run, Pallas kernels for 0% -> 0%
where the time goes in v2:
time: 38.9 us; the launch traced here: 38.8 us
  Pallas kernels  38.1 us (98%)
  between operations  0.64 us (2%)
    pallas_call x1, Pallas kernels, on_device(): pl.pallas_call(window, out_shape=(vm((C, S + 4, D, N), f32), vm((3, C, S...  36.6 us
    pallas_call x1, Pallas kernels, on_device(): pl.pallas_call(finish, out_shape=(shape((C, S, D, N), f32), shape((S, D,...  1.51 us

profile of v2, /device:TPU:1, one launch (start us, length us, event | category | flops | bytes accessed | tf_op | source)
XLA Modules:
  0.0 38.8 jit_solution(1467072600805202189)
XLA Ops:
  0.6 36.6 %window.1 = (f32[3,20,16,512]{3,2,1,0:T(8,128)S(1)}, f32[3,3,20,16,512]{4,3,2,1,0:T(8,128)S(1)}, f32[4,16,16,512]{3,2,1,0:T(8,128)S(1)}, f32[8,128]{1,0:T(8,128)S(1)}) custom-call(f32[3,16,16,512]{3,2,1,0:T(8,128)} %f_hbm.1, f32[3,16,16,512]{3,2,1,0:T(8,128)} %x_hbm.1, f32[16,16,512]{2,1,0:T(8,128)} %m_hbm.1, f32[3,256]{1,0:T(4,128)} %mis_hbm.1, ...), custom_call_target="tpu_custom_call" | custom-call | tf_op jit(solution)/shard_map/window/pallas_call | solution.py:624
  37.3 1.5 %finish.1 = (f32[3,16,16,512]{3,2,1,0:T(8,128)}, f32[16,16,512]{2,1,0:T(8,128)}) custom-call(f32[3,20,16,512]{3,2,1,0:T(8,128)S(1)} %get-tuple-element.6.xb, f32[3,3,20,16,512]{4,3,2,1,0:T(8,128)S(1)} %get-tuple-element.7.ub, f32[4,16,16,512]{3,2,1,0:T(8,128)S(1)} %get-tuple-element.8.gb, f32[8,128]{1,0:T(8,128)S(1)} %get-tuple-element.9.cv), custom_call_target="tpu_custom_call" | custom-call | tf_op jit(solution)/shard_map/finish/pallas_call | solution.py:644

commit v3 on v2

--- a/solution.py
+++ b/solution.py
@@ -11,7 +11,7 @@
 CAP = 8
 PENALTY = 4.0
 f32, bf16, i32 = jnp.float32, jnp.bfloat16, jnp.int32
-UNROLL = 4
+INNER, WHOLE = 14, 16
 
 
 def iota(shape, dim):
@@ -46,12 +46,12 @@
 
 
 def fold(v):
-    w = v[0:8, 128:N] + v[8:16, 128:N]
-    return w[:, 0:128] + w[:, 128:256] + w[:, 256:384]
+    w = v[0:8] + v[8:16]
+    return (w[:, 0:128] + w[:, 128:256]) + (w[:, 256:384] + w[:, 384:512])
 
 
 def window(f_hbm, x_hbm, m_hbm, mis_hbm, own_hbm, cell_hbm, xb, ub, gb, cv,
-           mb, fb, mf, xf, ff, uf, ms, xs, fs, us, mc, xc, uc, coef, diag, u3, wb, mis, own, cel,
+           mb, fb, mf, xf, ff, uf, ms, xs, fs, us, mc, xc, uc, coef, diag, inv, u3, wb, mis, own, cel,
            msg1, got1, msg2, got2, red, got3, got4,
            load_sem, ssem, rsem, cssem, crsem, wssem, wrsem, s1, r1, s2, r2, s3, r3, s4, r4):
     si, di = lax.axis_index("strike"), lax.axis_index("depth")
@@ -63,8 +63,8 @@
     not_first_d, not_last_d = di > 0, di < ND_DEV - 1
 
     loads = [pltpu.make_async_copy(src, dst, load_sem.at[j]) for j, (src, dst) in enumerate((
-        (mis_hbm, mis), (own_hbm, own), (cell_hbm, cel), (m_hbm, mb.at[pl.ds(2, S)]),
-        (x_hbm, xb.at[:, pl.ds(2, S)]), (f_hbm, fb.at[:, pl.ds(1, S)])))]
+        (mis_hbm, mis), (own_hbm, own), (cell_hbm, cel), (m_hbm, mb.at[pl.ds(2, S)]), (x_hbm.at[0], xb.at[0, pl.ds(2, S)]), (x_hbm.at[1], xb.at[1, pl.ds(2, S)]),
+        (x_hbm.at[2], xb.at[2, pl.ds(2, S)]), (f_hbm, fb.at[:, pl.ds(1, S)])))]
     for load in loads:
         load.start()
     wb[...] = jnp.zeros_like(wb)
@@ -84,82 +84,13 @@
     for t in greet:
         pl.semaphore_signal(barrier, inc=1, device_id=t, device_id_type=MESH)
 
-    for inside, planes, side in ((not_first_s, 0, 0), (not_last_s, S + 2, 1)):
-        @pl.when(jnp.logical_not(inside))
-        def _(planes=planes, side=side):
-            for j in range(2):
-                mb[planes + j] = jnp.zeros((D, N), f32)
-                for c in range(C):
-                    xb[c, planes + j] = jnp.zeros((D, N), f32)
-                    for k in range(3):
-                        ub[k, c, planes + j] = jnp.zeros((D, N), f32)
-            for c in range(C):
-                fb[c, (S + 1) * side] = jnp.zeros((D, N), f32)
-            for j in range(6):
-                coef[j, S + side] = jnp.zeros((D, N), f32)
-            mc[side] = jnp.zeros((2, 8, N), f32)
-            xc[side] = jnp.zeros((2, C, 8, N), f32)
-            uc[side] = jnp.zeros((2, C, 8, N), f32)
-    for inside, side in ((not_first_d, 0), (not_last_d, 1)):
-        @pl.when(jnp.logical_not(inside))
-        def _(side=side):
-            for j in range(6):
-                coef[j, S + 2 + side] = jnp.zeros((D, N), f32)
-            mf[side] = jnp.zeros((2, S, N), f32)
-            for c in range(C):
-                xf[c, side] = jnp.zeros((2, S, N), f32)
-                ff[c, side] = jnp.zeros((S, N), f32)
-                for k in range(3):
-                    uf[k, c, side] = jnp.zeros((2, S, N), f32)
-            for a in range(2):
-                mc[a, side] = jnp.zeros((8, N), f32)
-                xc[a, side] = jnp.zeros((C, 8, N), f32)
-                uc[a, side] = jnp.zeros((C, 8, N), f32)
-
-    for load in loads[:3]:
-        load.wait()
-    owner = own[...]
-    rows = owner.shape[1]
-    same = (iota((128, rows), 0) == owner).astype(f32)
-    before = (iota((rows, rows), 0) < iota((rows, rows), 1)).astype(f32).astype(bf16)
-    count = jnp.dot(same.astype(bf16), before, preferred_element_type=f32)
-    rank = jnp.sum(same * count, axis=0, keepdims=True)
-    place = owner * CAP + rank.astype(i32)
-    values = jnp.concatenate([mis[...], cel[...].astype(f32), jnp.zeros((4, rows), f32)], axis=0)
-    parts = jnp.concatenate([p.astype(f32) for p in thirds(values)], axis=0).astype(bf16)
-
-    def fill(q, _):
-        hot = (iota((128, rows), 0) + (q * 64 - 32) == place).astype(f32)
-        out = lax.dot_general(parts, hot.astype(bf16), (((1,), (1,)), ((), ())), preferred_element_type=f32)
-        msg1[q] = (out[0:8] + out[8:16] + out[16:24])[0:4]
-        return 0
-
-    lax.fori_loop(0, 16, fill, 0, unroll=4)
-
     def stage(read, to, layers):
-        for s in range(S):
-            v = read(s)
-            for layer in range(layers):
-                to[0, layer, s:s + 1] = v[layer:layer + 1]
-                to[1, layer, s:s + 1] = v[D - 1 - layer:D - layer]
-
-    loads[3].wait()
-    stage(lambda s: mb[s + 2], ms, 2)
-    col = iota((D, 128), 1)
-    for s in range(S):
-        tile = mb[s + 2, :, 0:128]
-        at = 4 * s + 16
-        mask = (col >= at) & (col < at + 4)
-        wb[1, 0, 8:24] += jnp.where(mask, pltpu.roll(tile, at, 1), 0.0)
-        wb[1, 1, 8:24] += jnp.where(mask, pltpu.roll(tile, at - 1, 1), 0.0)
-    loads[4].wait()
-    for c in range(C):
-        stage(lambda s, c=c: xb[c, s + 2], xs.at[c], 2)
-    loads[5].wait()
-    for c in range(C):
-        for s in range(S):
-            fs[c, 0, s:s + 1] = fb[c, s + 1, 0:1]
-            fs[c, 1, s:s + 1] = fb[c, s + 1, D - 1:D]
+        for g in range(0, S, 4):
+            got = [read(s) for s in range(g, g + 4)]
+            for j, v in enumerate(got):
+                for layer in range(layers):
+                    to[0, layer, g + j:g + j + 1] = v[layer:layer + 1]
+                    to[1, layer, g + j:g + j + 1] = v[D - 1 - layer:D - layer]
 
     def remote(src, dst, send_sem, recv_sem, t):
         return pltpu.make_async_remote_copy(src_ref=src, dst_ref=dst, send_sem=send_sem, recv_sem=recv_sem,
@@ -221,15 +152,13 @@
         return edges(0, mb, mf, ms) + corners(
             0, lambda side, row: ms.at[side, 0, pl.ds(row, 1)], lambda a, b: mc.at[a, b, pl.ds(0, 1)])
 
-    def x_corners():
-        return corners(1, lambda side, row: xs.at[:, side, 0, pl.ds(row, 1)], lambda a, b: xc.at[a, b, :, pl.ds(0, 1)])
-
     def x_edges(c):
-        return edges(1 + c, xb.at[c], xf.at[c], xs.at[c])
+        return edges(1 + c, xb.at[c], xf.at[c], xs.at[c]) + corners(
+            1 + c, lambda side, row: xs.at[c, side, 0, pl.ds(row, 1)], lambda a, b: xc.at[a, b, c, pl.ds(0, 1)])
 
     def u_edges(c):
         return edges(4 + c, ub.at[1, c], uf.at[1, c], us.at[c]) + corners(
-            2 + c, lambda side, row: us.at[c, side, 0, pl.ds(row, 1)], lambda a, b: uc.at[a, b, c, pl.ds(0, 1)])
+            4 + c, lambda side, row: us.at[c, side, 0, pl.ds(row, 1)], lambda a, b: uc.at[a, b, c, pl.ds(0, 1)])
 
     def send(copies):
         for has, _, copy in copies:
@@ -249,7 +178,7 @@
 
     def plane_copy(k):
         t, idx = near_dev(k)
-        return remote(msg2.at[idx], got2.at[near], s2.at[k], r2.at[k], t)
+        return remote(msg2.at[lax.rem(idx, 4)], got2.at[near], s2.at[k], r2.at[k], t)
 
     def sum_copy(k):
         t, _ = far_dev(k)
@@ -259,43 +188,181 @@
         t, _ = near_dev(k)
         return remote(red.at[1], got4.at[near], s4.at[k], r4.at[k], t)
 
+    for load in loads[:3]:
+        load.wait()
+    owner = own[...]
+    rows = owner.shape[1]
+    same = (iota((128, rows), 0) == owner).astype(f32)
+    before = (iota((rows, rows), 0) < iota((rows, rows), 1)).astype(f32).astype(bf16)
+    count = jnp.dot(same.astype(bf16), before, preferred_element_type=f32)
+    rank = jnp.sum(same * count, axis=0, keepdims=True)
+    place = owner * CAP + rank.astype(i32)
+    values = jnp.concatenate([mis[...], cel[...].astype(f32), jnp.zeros((4, rows), f32)], axis=0)
+    parts = jnp.concatenate([p.astype(f32) for p in thirds(values)], axis=0).astype(bf16)
+
+    def fill(q, _):
+        hot = (iota((128, rows), 0) + (q * 64 - 32) == place).astype(f32)
+        out = lax.dot_general(parts, hot.astype(bf16), (((1,), (1,)), ((), ())), preferred_element_type=f32)
+        msg1[q] = (out[0:8] + out[8:16] + out[16:24])[0:4]
+        return 0
+
+    lax.fori_loop(0, 16, fill, 0, unroll=4)
+
+    loads[3].wait()
+    stage(lambda s: mb[s + 2], ms, 2)
     pl.semaphore_wait(barrier, len(greet))
     send(m_edges())
-    send(x_corners())
     for c in range(C):
+        loads[4 + c].wait()
+        stage(lambda s, c=c: xb[c, s + 2], xs.at[c], 2)
         send(x_edges(c))
-        if c == 0:
-            for k in range(1, 16):
-                row_copy(k).start()
+
+    for k in range(1, 16):
+        row_copy(k).start()
+    got1[chip] = msg1[chip]
+    col = iota((D, 128), 1)
+    for s in range(S):
+        tile = mb[s + 2, :, 0:128]
+        at = 4 * s + 16
+        mask = (col >= at) & (col < at + 4)
+        wb[1, 0, 8:24] += jnp.where(mask, pltpu.roll(tile, at, 1), 0.0)
+        wb[1, 1, 8:24] += jnp.where(mask, pltpu.roll(tile, at - 1, 1), 0.0)
     send(patches())
-    got1[chip] = msg1[chip]
+
+    for inside, planes, side in ((not_first_s, 0, 0), (not_last_s, S + 2, 1)):
+        @pl.when(jnp.logical_not(inside))
+        def _(planes=planes, side=side):
+            for j in range(2):
+                mb[planes + j] = jnp.zeros((D, N), f32)
+                for c in range(C):
+                    xb[c, planes + j] = jnp.zeros((D, N), f32)
+                    for k in range(3):
+                        ub[k, c, planes + j] = jnp.zeros((D, N), f32)
+            for c in range(C):
+                fb[c, (S + 1) * side] = jnp.zeros((D, N), f32)
+            for j in range(6):
+                coef[j, S + side] = jnp.zeros((D, N), f32)
+            inv[S + side] = jnp.zeros((D, N), f32)
+            mc[side] = jnp.zeros((2, 8, N), f32)
+            xc[side] = jnp.zeros((2, C, 8, N), f32)
+            uc[side] = jnp.zeros((2, C, 8, N), f32)
+    for inside, side in ((not_first_d, 0), (not_last_d, 1)):
+        @pl.when(jnp.logical_not(inside))
+        def _(side=side):
+            for j in range(6):
+                coef[j, S + 2 + side] = jnp.zeros((D, N), f32)
+            inv[S + 2 + side] = jnp.zeros((D, N), f32)
+            mf[side] = jnp.zeros((2, S, N), f32)
+            for c in range(C):
+                xf[c, side] = jnp.zeros((2, S, N), f32)
+                ff[c, side] = jnp.zeros((S, N), f32)
+                for k in range(3):
+                    uf[k, c, side] = jnp.zeros((2, S, N), f32)
+            for a in range(2):
+                mc[a, side] = jnp.zeros((8, N), f32)
+                xc[a, side] = jnp.zeros((C, 8, N), f32)
+                uc[a, side] = jnp.zeros((C, 8, N), f32)
 
     first, last = iota((D, N), 1) == 0, iota((D, N), 1) == N - 1
+    none = jnp.zeros((D, N), f32)
+    no_row = jnp.zeros((1, N), f32)
 
     def coefs(p, m, low, high, row_low, row_high):
-        beside = [low, high, rows_low(m, row_low), rows_high(m, row_high),
-                  jnp.where(first, 0.0, cols_low(m)), jnp.where(last, 0.0, cols_high(m))]
+        beside = [low, high, rows_low(m, row_low), rows_high(m, row_high), cols_low(m), cols_high(m)]
         face = [0.5 * (m + b) for b in beside]
-        dd = jnp.where(first, PENALTY * m, 0.0)
-        for a in face:
+        dd = jnp.where(first, PENALTY * m + 0.5 * m, face[4]) + jnp.where(last, 0.5 * m, face[5])
+        for a in face[:4]:
             dd = dd + a
-        ii = 1.0 / dd
-        for j in range(6):
-            out = face[j] * ii
-            if j == 4:
-                out = jnp.where(first, 0.0, out)
-            if j == 5:
-                out = jnp.where(last, 0.0, out)
-            coef[j, p] = out
+        for j in range(4):
+            coef[j, p] = face[j]
+        coef[4, p] = jnp.where(first, 0.0, face[4])
+        coef[5, p] = jnp.where(last, 0.0, face[5])
         return dd
 
+    def put_diag(s, dd):
+        diag[s] = dd
+
+    def part_coefs(s, low, high):
+        return coefs(s, mb[s + 2], low, high, no_row, no_row)
+
+    def inner(work, put):
+        def step(g, _):
+            at = [1 + g * INNER + j for j in range(INNER)]
+            got = [work(s) for s in at]
+            for s, v in zip(at, got):
+                put(s, v)
+            return 0
+        lax.fori_loop(0, (S - 2) // INNER, step, 0)
+
+    def summed(first_plane, planes, work, put, sums):
+        group = WHOLE if planes == S else INNER
+
+        def step(g, sums):
+            at = [first_plane + g * group + j for j in range(group)]
+            got = [work(s) for s in at]
+            for s, (v, _) in zip(at, got):
+                put(s, v)
+            for _, terms in got:
+                sums = tuple(a + fold(t) for a, t in zip(sums, terms))
+            return sums
+        return lax.fori_loop(0, planes // group, step, sums)
+
+    put_diag(0, part_coefs(0, none, mb[3]))
+    put_diag(S - 1, part_coefs(S - 1, mb[S], none))
+    inner(lambda s: part_coefs(s, mb[s + 1], mb[s + 3]), put_diag)
+
+    def sweep(p, v, low, high, row_low, row_high):
+        out = coef[4, p] * cols_low(v) + coef[5, p] * cols_high(v)
+        out = out + coef[2, p] * rows_low(v, row_low) + coef[3, p] * rows_high(v, row_high)
+        if low is not None:
+            out = out + coef[0, p] * low
+        if high is not None:
+            out = out + coef[1, p] * high
+        return out
+
+    def part_field(planes, put):
+        put(0, sweep(0, planes(2), None, planes(3), no_row, no_row))
+        put(S - 1, sweep(S - 1, planes(S + 1), planes(S), None, no_row, no_row))
+        inner(lambda s: sweep(s, planes(s + 2), planes(s + 1), planes(s + 3), no_row, no_row), put)
+
+    top, bottom = iota((8, N), 0) == 0, iota((8, N), 0) == 7
+
+    def rest_of(s, w, faces, low, high):
+        up = w[0:8] + jnp.where(top, coef[2, s, 0:8] * faces(0, pl.ds(s, 1)), 0.0)
+        dn = w[8:16] + jnp.where(bottom, coef[3, s, 8:16] * faces(1, pl.ds(s, 1)), 0.0)
+        w = jnp.concatenate([up, dn], 0)
+        if low is not None:
+            w = w + coef[0, s] * low
+        if high is not None:
+            w = w + coef[1, s] * high
+        return w
+
+    def put_part(k, c):
+        def put(s, w):
+            ub[k, c, s + 2] = w
+        return put
+
+    for c in range(C):
+        part_field(lambda i, c=c: xb[c, i], put_part(0, c))
+
     recv(m_edges())
 
-    def own_coefs(s, _):
-        diag[s] = coefs(s, mb[s + 2], mb[s + 1], mb[s + 3], mf[0, 0, pl.ds(s, 1)], mf[1, 0, pl.ds(s, 1)])
-        return 0
-
-    lax.fori_loop(0, S, own_coefs, 0, unroll=2)
+    def rest_coefs(s, low, high):
+        up, dn = 0.5 * mf[0, 0, pl.ds(s, 1)], 0.5 * mf[1, 0, pl.ds(s, 1)]
+        up, dn = jnp.where(top, up, 0.0), jnp.where(bottom, dn, 0.0)
+        coef[2, s, 0:8] += up
+        coef[3, s, 8:16] += dn
+        dd = diag[s] + jnp.concatenate([up, dn], 0)
+        for j, halo in ((0, low), (1, high)):
+            if halo is not None:
+                coef[j, s] += 0.5 * halo
+                dd = dd + 0.5 * halo
+        diag[s] = dd
+        inv[s] = 1.0 / dd
+
+    rest_coefs(0, mb[1], None)
+    rest_coefs(S - 1, None, mb[S + 2])
+    inner(lambda s: rest_coefs(s, None, None), lambda s, v: None)
     outer = [not_first_s, not_last_s, not_first_d, not_last_d]
 
     def corner(cells, a, b):
@@ -313,16 +380,11 @@
                                          lambda a, b: mc[a, b])):
         @pl.when(outer[j])
         def _(j=j, get=get):
-            coefs(S + j, *get())
-
-    def sweep(p, v, low, high, row_low, row_high):
-        out = coef[0, p] * low + coef[1, p] * high
-        out = out + coef[2, p] * rows_low(v, row_low) + coef[3, p] * rows_high(v, row_high)
-        return out + coef[4, p] * cols_low(v) + coef[5, p] * cols_high(v)
+            inv[S + j] = 1.0 / coefs(S + j, *get())
 
     def own_sweep(planes, faces, s):
         v = planes(s + 2)
-        return v, sweep(s, v, planes(s + 1), planes(s + 3), faces(0, pl.ds(s, 1)), faces(1, pl.ds(s, 1)))
+        return v, inv[s] * sweep(s, v, planes(s + 1), planes(s + 3), faces(0, pl.ds(s, 1)), faces(1, pl.ds(s, 1)))
 
     def keep_outer(k, c, j, v):
         if j == 0:
@@ -337,33 +399,39 @@
     sums1 = (zero8,) * 2
     sums2 = (zero8,)
 
-    recv(x_corners())
-
     def first_half(c, sums):
         recv(x_edges(c))
 
-        def start_field(s, _):
-            v, w = own_sweep(lambda i: xb[c, i], lambda a, r: xf[c, a, 0, r], s)
-            ub[0, c, s + 2] = w - v
-            return 0
-
-        lax.fori_loop(0, S, start_field, 0, unroll=UNROLL)
+        def start_field(s, low, high):
+            w = rest_of(s, ub[0, c, s + 2], lambda a, r: xf[c, a, 0, r], low, high)
+            return inv[s] * w - xb[c, s + 2]
+
+        put = put_part(0, c)
+        ends = start_field(0, xb[c, 1], None), start_field(S - 1, None, xb[c, S + 2])
+        put(0, ends[0])
+        put(S - 1, ends[1])
+        inner(lambda s: start_field(s, None, None), put)
+        made = []
         for j, get in enumerate(outer_planes(lambda i: xb[c, i], lambda a, b: xf[c, a, b], lambda a: xs[c, a, 0],
                                              lambda a, b: xc[a, b, c])):
             got = get()
-            keep_outer(0, c, j, sweep(S + j, *got) - got[0])
-
-        def step(s, sums):
+            made.append(inv[S + j] * sweep(S + j, *got) - got[0])
+        for j, v in enumerate(made):
+            keep_outer(0, c, j, v)
+
+        def step(s):
             v, w = own_sweep(lambda i: ub[0, c, i], lambda a, r: uf[0, c, a, 0, r], s)
+            dd = diag[s]
+            de = dd * (v - w)
+            return w, (dd * v * v, de * v, de * w)
+
+        def put_next(s, w):
             ub[1, c, s + 2] = w
             for layer in range(2):
                 us[c, 0, layer, pl.ds(s, 1)] = w[layer:layer + 1]
                 us[c, 1, layer, pl.ds(s, 1)] = w[D - 1 - layer:D - layer]
-            dd = diag[s]
-            de = dd * (v - w)
-            return (sums[0] + fold(dd * v * v), sums[1] + fold(de * v), sums[2] + fold(de * w))
-
-        sums = lax.fori_loop(0, S, step, sums, unroll=UNROLL)
+
+        sums = summed(0, S, step, put_next, sums)
         send(u_edges(c))
         return sums
 
@@ -382,13 +450,9 @@
             at_s, at_d = brick_s * S + at // D, brick_d * D + lax.rem(at, D) + 8
             hot_d.append((iota((80, 128), 0) == at_d).astype(f32))
             vals = [p.astype(f32) for p in thirds(row)]
-            hits = [iota((32, 128), 0) == at_s + (4 - S * o) for o in range(2)]
+            hit = iota((40, 128), 0) == at_s + 4
             for part in range(3):
-                lines = []
-                for o in range(2):
-                    for c in range(C):
-                        lines.append(jnp.where(hits[o], vals[part][c:c + 1], 0.0))
-                    lines.append(jnp.zeros((32, 128), f32))
+                lines = [jnp.where(hit, vals[part][c:c + 1], 0.0) for c in range(C)] + [jnp.zeros((8, 128), f32)]
                 right[part].append(jnp.concatenate(lines, axis=0))
         left = jnp.concatenate(hot_d, axis=1).astype(bf16)
         for part in range(3):
@@ -396,18 +460,26 @@
                                             (((1,), (1,)), ((), ())), preferred_element_type=f32)
         return total
 
-    dense = jnp.zeros((80, 256), f32)
+    dense = jnp.zeros((80, 128), f32)
     for half in range(4):
         dense = plane_part(half, dense)
-    for t in range(8):
-        msg2[t] = dense[(t % 4) * D:(t % 4) * D + 32, (t // 4) * 128:(t // 4 + 1) * 128]
+    for t in range(4):
+        msg2[t] = dense[t * D:t * D + 32]
     for k in range(1, 8):
         plane_copy(k).start()
-    got2[near] = msg2[near]
+    got2[near] = msg2[di]
 
     for c in range(1, C):
         sums0 = first_half(c, sums0)
+    loads[7].wait()
+    for c in range(C):
+        for s in range(S):
+            fs[c, 0, s:s + 1] = fb[c, s + 1, 0:1]
+            fs[c, 1, s:s + 1] = fb[c, s + 1, D - 1:D]
+
     send(forward_edges())
+    for c in range(C):
+        part_field(lambda i, c=c: ub[1, c, i], put_part(2, c))
 
     recv(patches())
     lane = iota((32, 128), 1)
@@ -434,26 +506,36 @@
     def second_half(c, sums1, sums2):
         recv(u_edges(c))
 
-        def step(s, sums):
-            v, w = own_sweep(lambda i: ub[1, c, i], lambda a, r: uf[1, c, a, 0, r], s)
-            ub[2, c, s + 2] = w
+        def step(s, low, high):
+            v = ub[1, c, s + 2]
+            w = inv[s] * rest_of(s, ub[2, c, s + 2], lambda a, r: uf[1, c, a, 0, r], low, high)
             de = diag[s] * (v - w)
-            return (sums[0] + fold(de * v), sums[1] + fold(de * w))
-
-        sums1 = lax.fori_loop(0, S, step, sums1, unroll=UNROLL)
+            return w, (de * v, de * w)
+
+        put = put_part(2, c)
+        ends = step(0, ub[1, c, 1], None), step(S - 1, None, ub[1, c, S + 2])
+        for s, (w, terms) in zip((0, S - 1), ends):
+            put(s, w)
+            sums1 = tuple(a + fold(t) for a, t in zip(sums1, terms))
+        sums1 = summed(1, S - 2, lambda s: step(s, None, None), put, sums1)
+        made = []
         for j, get in enumerate(outer_planes(lambda i: ub[1, c, i], lambda a, b: uf[1, c, a, b],
                                              lambda a: us[c, a, 0], lambda a, b: uc[a, b, c])):
-            keep_outer(2, c, j, sweep(S + j, *get()))
-
-        def final(s, sums):
+            made.append(inv[S + j] * sweep(S + j, *get()))
+        for j, v in enumerate(made):
+            keep_outer(2, c, j, v)
+
+        def final(s):
             v, w = own_sweep(lambda i: ub[2, c, i], lambda a, r: uf[2, c, a, 0, r], s)
-            u3[c, s] = w[:, 0:128]
-            return (sums[0] + fold(diag[s] * v * (v - w)),)
-
-        sums2 = lax.fori_loop(0, S, final, sums2, unroll=UNROLL)
+            return w[:, 0:128], (diag[s] * v * (v - w),)
+
+        def put_final(s, w):
+            u3[c, s] = w
+
+        sums2 = summed(0, S, final, put_final, sums2)
         return sums1, sums2
 
-    for c in range(C):
+    for c in range(2):
         sums1, sums2 = second_half(c, sums1, sums2)
 
     for k in range(1, 8):
@@ -461,8 +543,10 @@
     plane = got2[0]
     for j in range(1, 8):
         plane = plane + got2[j]
-    spread = ((iota((128, 384), 0) // 32 == iota((128, 384), 1) // 128)
-              & (lax.rem(iota((128, 384), 0), 32) * 4 == lax.rem(iota((128, 384), 1), 128))).astype(f32).astype(bf16)
+    strike_at = lax.rem(iota((128, 128), 0), 40) - S * core
+    spread = jnp.concatenate([
+        ((iota((128, 128), 0) // 40 == c) & (strike_at < 24) & (strike_at * 4 == iota((128, 128), 1))).astype(f32)
+        for c in range(C)], axis=1).astype(bf16)
     left = jnp.concatenate([p.astype(f32) for p in thirds(plane)], axis=0).astype(bf16)
     out = jnp.dot(left, spread, preferred_element_type=f32)
     out = out[0:32] + out[32:64] + out[64:96]
@@ -484,25 +568,30 @@
     def fold_near(v):
         return v[0:8] + v[8:16]
 
-    for c in range(C):
-        sent(u_edges(c))
-    sums0, sums1, sums2 = list(sums0), list(sums1), list(sums2)
-    for s in range(S):
-        dd = diag[s, :, 0:128]
-        for c in range(C):
-            v = []
-            for k in range(3):
-                v.append(ub[k, c, s + 2, :, 0:128] + share(k, c, s + 2))
-                ub[k, c, s + 2, :, 0:128] = v[k]
-            v.append(u3[c, s] + share(3, c, s + 2))
-            de = [dd * (v[k] - v[k + 1]) for k in range(3)]
-            sums0[0] = sums0[0] + fold_near(dd * v[0] * v[0])
-            sums0[1] = sums0[1] + fold_near(de[0] * v[0])
-            sums0[2] = sums0[2] + fold_near(de[0] * v[1])
-            sums1[0] = sums1[0] + fold_near(de[1] * v[1])
-            sums1[1] = sums1[1] + fold_near(de[1] * v[2])
-            sums2[0] = sums2[0] + fold_near(de[2] * v[2])
-    sums = sums0 + sums1 + sums2
+    weight = jnp.where((col >= 16) & (col < 80), total[8:24], 0.0)
+
+    def gather(k, c):
+        out = jnp.zeros((D, 128), f32)
+        for s in range(S):
+            tile = u3[c, s] if k == 3 else ub[k, c, s + 2, :, 0:128]
+            out = jnp.where(col // 4 == s + 4, pltpu.roll(tile, 4 * s + 16, 1), out)
+        return out
+
+    def products(v):
+        de = [weight * (v[k] - v[k + 1]) for k in range(3)]
+        return [weight * v[0] * v[0], de[0] * v[0], de[0] * v[1], de[1] * v[1], de[1] * v[2], de[2] * v[2]]
+
+    def change(c, sums):
+        v = [gather(k, c) for k in range(4)]
+        new = products([v[k] + shares[k][c][8:24] for k in range(4)])
+        return [a + fold_near(p - q) for a, p, q in zip(sums, new, products(v))]
+
+    sums = [zero8] * 6
+    for c in range(2):
+        sums = change(c, sums)
+    sums1, sums2 = second_half(2, sums1, sums2)
+    sums = change(2, sums)
+    sums = [a + b for a, b in zip(sums, sums0 + sums1 + sums2)]
     for j in range(6):
         red[0, j:j + 1] = jnp.sum(sums[j], axis=0, keepdims=True)
     red[0, 6:8] = jnp.zeros((2, 128), f32)
@@ -510,16 +599,29 @@
     for k in range(1, 16):
         sum_copy(k).start()
     got3[chip] = red[0]
+    for c in range(C):
+        sent(u_edges(c))
     for k in range(3):
         for c in range(C):
-            for i in (1, S + 2):
-                ub[k, c, i, :, 0:128] += share(k, c, i)
-            for side, r in ((0, 7), (1, 24)):
-                row = jnp.broadcast_to(shares[k][c][r:r + 1], (S, 128))
-                row = pltpu.roll(row, 128 - 16, 1)
-                for bit in (1, 2, 4, 8):
-                    row = jnp.where(iota((S, 128), 0) & bit > 0, pltpu.roll(row, 128 - 4 * bit, 1), row)
-                uf[k, c, side, 0, :, 0:128] += jnp.where(few, row, 0.0)
+            for g in range(1, S + 3, 18):
+                new = [ub[k, c, i, :, 0:128] + share(k, c, i) for i in range(g, g + 18)]
+                for j, v in enumerate(new):
+                    ub[k, c, g + j, :, 0:128] = v
+
+    @pl.when(si >= 0)
+    def _():
+        rows = []
+        for k in range(3):
+            for c in range(C):
+                for side, r in ((0, 7), (1, 24)):
+                    row = jnp.broadcast_to(shares[k][c][r:r + 1], (S, 128))
+                    row = pltpu.roll(row, 128 - 16, 1)
+                    for bit in (1, 2, 4, 8):
+                        row = jnp.where(iota((S, 128), 0) & bit > 0, pltpu.roll(row, 128 - 4 * bit, 1), row)
+                    rows.append(uf[k, c, side, 0, :, 0:128] + jnp.where(few, row, 0.0))
+        for j, row in enumerate(rows):
+            uf[j // (2 * C), (j // 2) % C, j % 2, 0, :, 0:128] = row
+
     recv(forward_edges())
 
     start, end = iota((D, 128), 1) == 0, iota((D, 128), 1) == 127
@@ -549,7 +651,7 @@
             gb[k, s] = -0.25 * total[k]
         return 0
 
-    lax.fori_loop(0, S // 2, gradients, 0)
+    lax.fori_loop(0, S // 2, gradients, 0, unroll=2)
     for k in range(1, 16):
         sum_copy(k).wait_recv()
     part = got3[0]
@@ -559,9 +661,8 @@
     for k in range(1, 8):
         last_copy(k).start()
     got4[near] = part
-    lax.fori_loop(S // 2, S, gradients, 0)
+    lax.fori_loop(S // 2, S, gradients, 0, unroll=2)
     sent(m_edges())
-    sent(x_corners())
     sent(patches())
     sent(forward_edges())
     for c in range(C):
@@ -631,11 +732,11 @@
             vm((2, 2, S, N), f32), vm((C, 2, 2, S, N), f32), vm((C, 2, S, N), f32), vm((3, C, 2, 2, S, N), f32),
             vm((2, 2, S, N), f32), vm((C, 2, 2, S, N), f32), vm((C, 2, S, N), f32), vm((C, 2, 2, S, N), f32),
             vm((2, 2, 8, N), f32), vm((2, 2, C, 8, N), f32), vm((2, 2, C, 8, N), f32),
-            vm((6, S + 4, D, N), f32), vm((S, D, N), f32), vm((C, S, D, 128), f32), vm((3, 2, 32, 128), f32),
+            vm((6, S + 4, D, N), f32), vm((S, D, N), f32), vm((S + 4, D, N), f32), vm((C, S, D, 128), f32), vm((3, 2, 32, 128), f32),
             vm((C, rows), f32), vm((1, rows), i32), vm((1, rows), i32),
-            vm((16, 4, 128), f32), vm((16, 4, 128), f32), vm((8, 32, 128), f32), vm((8, 32, 128), f32),
+            vm((16, 4, 128), f32), vm((16, 4, 128), f32), vm((4, 32, 128), f32), vm((8, 32, 128), f32),
             vm((2, 8, 128), f32), vm((16, 8, 128), f32), vm((8, 8, 128), f32),
-            dma((6,)), dma((8, 4)), dma((8, 4)), dma((5, 4)), dma((5, 4)), dma((8,)), dma((8,)),
+            dma((8,)), dma((8, 4)), dma((8, 4)), dma((7, 4)), dma((7, 4)), dma((8,)), dma((8,)),
             dma((16,)), dma((16,)), dma((8,)), dma((8,)), dma((16,)), dma((16,)), dma((8,)), dma((8,)),
         ],
         compiler_params=pltpu.CompilerParams(collective_id=0, has_side_effects=True, vmem_limit_bytes=40 << 20),

time: 38.9 us -> 37.6 us (0.967)
  Pallas kernels: 38.1 us -> 36.7 us
    pallas_call x1, Pallas kernels: 36.6 us -> 35.2 us  [on_device(): pl.pallas_call(window, out_shape=(vm((C, S + 4, D, N), f32), vm((3, C, S...]
where the time goes in v3:
time: 37.6 us; the launch traced here: 37.5 us
  Pallas kernels  36.7 us (98%)
  between operations  0.8 us (2%)
    pallas_call x1, Pallas kernels, on_device(): pl.pallas_call(window, out_shape=(vm((C, S + 4, D, N), f32), vm((3, C, S...  35.2 us
    pallas_call x1, Pallas kernels, on_device(): pl.pallas_call(finish, out_shape=(shape((C, S, D, N), f32), shape((S, D,...  1.51 us

profile of v3, /device:TPU:1, one launch (start us, length us, event | category | flops | bytes accessed | tf_op | source)
XLA Modules:
  0.0 37.5 jit_solution(2912925993273479228)
XLA Ops:
  0.6 35.2 %window.1 = (f32[3,20,16,512]{3,2,1,0:T(8,128)S(1)}, f32[3,3,20,16,512]{4,3,2,1,0:T(8,128)S(1)}, f32[4,16,16,512]{3,2,1,0:T(8,128)S(1)}, f32[8,128]{1,0:T(8,128)S(1)}) custom-call(f32[3,16,16,512]{3,2,1,0:T(8,128)} %f_hbm.1, f32[3,16,16,512]{3,2,1,0:T(8,128)} %x_hbm.1, f32[16,16,512]{2,1,0:T(8,128)} %m_hbm.1, f32[3,256]{1,0:T(4,128)} %mis_hbm.1, ...), custom_call_target="tpu_custom_call" | custom-call | tf_op jit(solution)/shard_map/window/pallas_call | solution.py:725
  35.8 1.5 %finish.1 = (f32[3,16,16,512]{3,2,1,0:T(8,128)}, f32[16,16,512]{2,1,0:T(8,128)}) custom-call(f32[3,20,16,512]{3,2,1,0:T(8,128)S(1)} %get-tuple-element.6.xb, f32[3,3,20,16,512]{4,3,2,1,0:T(8,128)S(1)} %get-tuple-element.7.ub, f32[4,16,16,512]{3,2,1,0:T(8,128)S(1)} %get-tuple-element.8.gb, f32[8,128]{1,0:T(8,128)S(1)} %get-tuple-element.9.cv), custom_call_target="tpu_custom_call" | custom-call | tf_op jit(solution)/shard_map/finish/pallas_call | solution.py:745

commit v4 on v3

--- a/solution.py
+++ b/solution.py
@@ -212,13 +212,13 @@
     stage(lambda s: mb[s + 2], ms, 2)
     pl.semaphore_wait(barrier, len(greet))
     send(m_edges())
+    for k in range(1, 16):
+        row_copy(k).start()
     for c in range(C):
         loads[4 + c].wait()
         stage(lambda s, c=c: xb[c, s + 2], xs.at[c], 2)
         send(x_edges(c))
 
-    for k in range(1, 16):
-        row_copy(k).start()
     got1[chip] = msg1[chip]
     col = iota((D, 128), 1)
     for s in range(S):

time: 37.6 us -> 36.8 us (0.979)
  Pallas kernels: 36.7 us -> 35.9 us
    pallas_call x1, Pallas kernels: 35.2 us -> 34.4 us  [on_device(): pl.pallas_call(window, out_shape=(vm((C, S + 4, D, N), f32), vm((3, C, S...]
where the time goes in v4:
time: 36.8 us; the launch traced here: 36.7 us
  Pallas kernels  35.9 us (98%)
  between operations  0.8 us (2%)
    pallas_call x1, Pallas kernels, on_device(): pl.pallas_call(window, out_shape=(vm((C, S + 4, D, N), f32), vm((3, C, S...  34.4 us
    pallas_call x1, Pallas kernels, on_device(): pl.pallas_call(finish, out_shape=(shape((C, S, D, N), f32), shape((S, D,...  1.51 us

profile of v4, /device:TPU:1, one launch (start us, length us, event | category | flops | bytes accessed | tf_op | source)
XLA Modules:
  0.0 36.7 jit_solution(10589626795159112184)
XLA Ops:
  0.6 34.4 %window.1 = (f32[3,20,16,512]{3,2,1,0:T(8,128)S(1)}, f32[3,3,20,16,512]{4,3,2,1,0:T(8,128)S(1)}, f32[4,16,16,512]{3,2,1,0:T(8,128)S(1)}, f32[8,128]{1,0:T(8,128)S(1)}) custom-call(f32[3,16,16,512]{3,2,1,0:T(8,128)} %f_hbm.1, f32[3,16,16,512]{3,2,1,0:T(8,128)} %x_hbm.1, f32[16,16,512]{2,1,0:T(8,128)} %m_hbm.1, f32[3,256]{1,0:T(4,128)} %mis_hbm.1, ...), custom_call_target="tpu_custom_call" | custom-call | tf_op jit(solution)/shard_map/window/pallas_call | solution.py:725
  35.1 1.5 %finish.1 = (f32[3,16,16,512]{3,2,1,0:T(8,128)}, f32[16,16,512]{2,1,0:T(8,128)}) custom-call(f32[3,20,16,512]{3,2,1,0:T(8,128)S(1)} %get-tuple-element.6.xb, f32[3,3,20,16,512]{4,3,2,1,0:T(8,128)S(1)} %get-tuple-element.7.ub, f32[4,16,16,512]{3,2,1,0:T(8,128)S(1)} %get-tuple-element.8.gb, f32[8,128]{1,0:T(8,128)S(1)} %get-tuple-element.9.cv), custom_call_target="tpu_custom_call" | custom-call | tf_op jit(solution)/shard_map/finish/pallas_call | solution.py:745
